TPU v7x, 32 devices: a whole 2x2x4 slice. The times are simulated.
32 devices in a mesh: dp: 1, seq: 32 (over z, y, x, core).
Axes of the slice: x: 2, y: 2, z: 4, core: 2. Of those that a mesh axis runs over, the one named last changes fastest.
Arguments:
- queries: bfloat16 [1, 4096, 1024], P('dp', 'seq'), may hold values from -6 to 6
- keys: bfloat16 [1, 4096, 1024], P('dp', 'seq'), may hold values from -6 to 6
- values: bfloat16 [1, 4096, 1024], P('dp', 'seq'), may hold values from -6 to 6
- gates: bfloat16 [1, 4096, 1024], P('dp', 'seq'), may hold values from -6 to 6
- cotangent: bfloat16 [1, 4096, 1024], P('dp', 'seq'), may hold values from -6 to 6
- segment: int32 [1, 4096], P('dp'), may hold values from 0 to 15, never falling along the last dimension, each value on 1 to 1024 neighbouring positions
- w_out: bfloat16 [1024, 1024], replicated, may hold values from -0.1875 to 0.1875
Outputs:
- output: bfloat16 [1, 4096, 1024], P('dp', 'seq')
- grad_queries: bfloat16 [1, 4096, 1024], P('dp', 'seq')
- grad_keys: bfloat16 [1, 4096, 1024], P('dp', 'seq')
- grad_values: bfloat16 [1, 4096, 1024], P('dp', 'seq')
- grad_gates: bfloat16 [1, 4096, 1024], P('dp', 'seq')
- grad_w_out: float32 [1024, 1024], P(('dp', 'seq'))
Inputs may be any that keep to these rules, and one draw needn't show every extreme that they name: `segment`: within each replica the user numbers never fall along the tokens; every user has 1 to 1024 tokens, and one user has exactly 1024.
All inputs are finite; a program needn't handle non-finite values.
Results may differ from a plain program's by a relative error of at most 0.0058.
Values may be sent and summed in bfloat16 or wider, within the bound.
A program may use at most 128 MiB of HBM per device.

v0:
```python
import math

import jax
import jax.numpy as jnp
from jax import lax
from jax.sharding import PartitionSpec as P

HEADS = 8
HOPS = 8


EPS = 1e-05


def from_behind(block, axis, distance):
    devices = range(lax.axis_size(axis))
    route = [(i - distance, i) for i in devices if i - distance in devices]
    return lax.ppermute(block, axis, route)


def silu_slope(scores):
    sigmoid_value = jax.nn.sigmoid(scores)
    return sigmoid_value * (1.0 + scores * (1.0 - sigmoid_value))


def block_pass(query_rows, gate_rows, cotan_rows, w_out, key_rows, value_rows, allowed):
    row_count, features = query_rows.shape
    head_size = features // HEADS
    score_scale = 1.0 / math.sqrt(head_size)
    query_heads = query_rows.reshape(row_count, HEADS, head_size)
    key_heads = key_rows.reshape(-1, HEADS, head_size)
    value_heads = value_rows.reshape(-1, HEADS, head_size)
    scores = (
        jnp.einsum("qhd,khd->hqk", query_heads, key_heads, preferred_element_type=jnp.float32)
        * score_scale
    )
    weights = jnp.where(allowed[None], jax.nn.silu(scores), 0.0).astype(jnp.bfloat16)
    mixed = jnp.einsum(
        "hqk,khd->qhd", weights, value_heads, preferred_element_type=jnp.float32
    ).reshape(row_count, features)
    row_mean = jnp.mean(mixed, axis=-1, keepdims=True)
    centred = mixed - row_mean
    inverse = lax.rsqrt(jnp.mean(centred * centred, axis=-1, keepdims=True) + EPS)
    normed = centred * inverse
    gate_float = gate_rows.astype(jnp.float32)
    gated = (normed * gate_float).astype(jnp.bfloat16)
    output_rows = jnp.dot(gated, w_out, preferred_element_type=jnp.float32).astype(jnp.bfloat16)
    dgated = jnp.einsum("rc,wc->rw", cotan_rows, w_out, preferred_element_type=jnp.float32)
    grad_gate_rows = (dgated * normed).astype(jnp.bfloat16)
    dnormed = dgated * gate_float
    dmixed = inverse * (
        dnormed
        - jnp.mean(dnormed, axis=-1, keepdims=True)
        - normed * jnp.mean(dnormed * normed, axis=-1, keepdims=True)
    )
    dmixed_heads = dmixed.astype(jnp.bfloat16).reshape(row_count, HEADS, head_size)
    dweights = jnp.einsum(
        "qhd,khd->hqk", dmixed_heads, value_heads, preferred_element_type=jnp.float32
    )
    dscores = jnp.where(allowed[None], dweights * silu_slope(scores) * score_scale, 0.0).astype(
        jnp.bfloat16
    )
    dvalue_rows = jnp.einsum(
        "hqk,qhd->khd", weights, dmixed_heads, preferred_element_type=jnp.float32
    ).reshape(-1, features)
    dquery_rows = jnp.einsum(
        "hqk,khd->qhd", dscores, key_heads, preferred_element_type=jnp.float32
    ).reshape(row_count, features)
    dkey_rows = jnp.einsum(
        "hqk,qhd->khd", dscores, query_heads, preferred_element_type=jnp.float32
    ).reshape(-1, features)
    weight_part = jnp.einsum("rw,rc->wc", gated, cotan_rows, preferred_element_type=jnp.float32)
    return (
        output_rows,
        dquery_rows.astype(jnp.bfloat16),
        grad_gate_rows,
        dkey_rows,
        dvalue_rows,
        weight_part,
    )


def shards(queries, keys, values, gates, cotangent, segment, w_out):
    query_rows = queries[0]
    gate_rows = gates[0]
    cotan_rows = cotangent[0]
    segment_ids = segment[0]
    row_count, features = query_rows.shape
    reach_rows = HOPS * row_count
    key_count = reach_rows + row_count
    device_index = lax.axis_index("seq")
    first_row = device_index * row_count
    own_block = jnp.stack([keys[0], values[0]])
    arrived = [own_block]
    moving = own_block
    for distance in range(1, HOPS + 1):
        moving = from_behind(moving, "seq", 1)
        arrived.append(moving)
    ordered = arrived[::-1]
    key_rows = jnp.concatenate([block[0] for block in ordered])
    value_rows = jnp.concatenate([block[1] for block in ordered])
    segment_padded = jnp.concatenate([jnp.full((reach_rows,), -1, jnp.int32), segment_ids])
    key_segment = lax.dynamic_slice_in_dim(segment_padded, first_row, key_count)
    query_segment = lax.dynamic_slice_in_dim(segment_ids, first_row, row_count)
    query_place = first_row + jnp.arange(row_count, dtype=jnp.int32)
    key_place = first_row - reach_rows + jnp.arange(key_count, dtype=jnp.int32)
    allowed = (query_segment[:, None] == key_segment[None, :]) & (
        key_place[None, :] <= query_place[:, None]
    )
    output_rows, dquery_rows, grad_gate_rows, dkey_rows, dvalue_rows, weight_part = block_pass(
        query_rows, gate_rows, cotan_rows, w_out, key_rows, value_rows, allowed
    )
    grads_all = jnp.stack([dkey_rows, dvalue_rows])

    def share_of(distance):
        return grads_all[:, (HOPS - distance) * row_count : (HOPS - distance + 1) * row_count]

    summed = share_of(HOPS)
    for distance in range(HOPS - 1, -1, -1):
        summed = from_behind(summed, "seq", -1) + share_of(distance)
    weight_grad = lax.psum_scatter(weight_part, ("dp", "seq"), scatter_dimension=0, tiled=True)
    return (
        output_rows[None],
        dquery_rows[None],
        summed[0].astype(jnp.bfloat16)[None],
        summed[1].astype(jnp.bfloat16)[None],
        grad_gate_rows[None],
        weight_grad,
    )


def solution(mesh):
    placed = (
        P("dp", "seq", None),
        P("dp", "seq", None),
        P("dp", "seq", None),
        P("dp", "seq", None),
        P("dp", "seq", None),
        P("dp", None),
        P(),
    )
    return jax.shard_map(
        shards,
        mesh=mesh,
        in_specs=placed,
        out_specs=(
            P("dp", "seq", None),
            P("dp", "seq", None),
            P("dp", "seq", None),
            P("dp", "seq", None),
            P("dp", "seq", None),
            P(("dp", "seq"), None),
        ),
        check_vma=False,
    )
```

profile of v0, /device:TPU:0, one launch (start us, length us, event | category | flops | bytes accessed | tf_op | source)
XLA Modules:
  0.0 366.8 jit_solution(1549842260759175291)
XLA Ops:
  9.7 2.4 collective-permute-start
  13.6 9.1 %collective-permute-start.1 = (bf16[2,128,1024]{1,2,0:T(8,128)(2,1)S(1)}, bf16[2,128,1024]{1,2,0:T(8,128)(2,1)S(1)}, u32[]{:S(2)}, u32[]{:S(2)}) collective-permute-start(bf16[2,128,1024]{1,2,0:T(8,128)(2,1)S(1)} %collective-permute-done), channel_id=1, source_target_pairs={{0,1},{1,2},{2,3},{3,4},{4,5},{5,6},{6,7},{7,8},{8,9},{9,10},{10,1... | collective-permute-start | bytes 1572872 | tf_op jit(solution)/shard_map/ppermute | solution.py:18
  25.0 9.0 %collective-permute-start.2 = (bf16[2,128,1024]{1,2,0:T(8,128)(2,1)S(1)}, bf16[2,128,1024]{1,2,0:T(8,128)(2,1)S(1)}, u32[]{:S(2)}, u32[]{:S(2)}) collective-permute-start(bf16[2,128,1024]{1,2,0:T(8,128)(2,1)S(1)} %collective-permute-done.1), channel_id=1, source_target_pairs={{0,1},{1,2},{2,3},{3,4},{4,5},{5,6},{6,7},{7,8},{8,9},{9,10},{10,1... | collective-permute-start | bytes 1572872 | tf_op jit(solution)/shard_map/ppermute | solution.py:18
  36.3 9.0 %collective-permute-start.3 = (bf16[2,128,1024]{1,2,0:T(8,128)(2,1)S(1)}, bf16[2,128,1024]{1,2,0:T(8,128)(2,1)S(1)}, u32[]{:S(2)}, u32[]{:S(2)}) collective-permute-start(bf16[2,128,1024]{1,2,0:T(8,128)(2,1)S(1)} %collective-permute-done.2), channel_id=1, source_target_pairs={{0,1},{1,2},{2,3},{3,4},{4,5},{5,6},{6,7},{7,8},{8,9},{9,10},{10,1... | collective-permute-start | bytes 1572872 | tf_op jit(solution)/shard_map/ppermute | solution.py:18
  46.8 9.8 %collective-permute-start.4 = (bf16[2,128,1024]{1,2,0:T(8,128)(2,1)S(1)}, bf16[2,128,1024]{1,2,0:T(8,128)(2,1)}, u32[]{:S(2)}, u32[]{:S(2)}) collective-permute-start(bf16[2,128,1024]{1,2,0:T(8,128)(2,1)S(1)} %collective-permute-done.3), channel_id=1, source_target_pairs={{0,1},{1,2},{2,3},{3,4},{4,5},{5,6},{6,7},{7,8},{8,9},{9,10},{10,1... | collective-permute-start | bytes 1572872 | tf_op jit(solution)/shard_map/ppermute | solution.py:18
  58.0 9.0 %collective-permute-start.5 = (bf16[2,128,1024]{1,2,0:T(8,128)(2,1)}, bf16[2,128,1024]{1,2,0:T(8,128)(2,1)}, u32[]{:S(2)}, u32[]{:S(2)}) collective-permute-start(bf16[2,128,1024]{1,2,0:T(8,128)(2,1)} %collective-permute-done.4), channel_id=1, source_target_pairs={{0,1},{1,2},{2,3},{3,4},{4,5},{5,6},{6,7},{7,8},{8,9},{9,10},{10,1... | collective-permute-start | bytes 1572872 | tf_op jit(solution)/shard_map/ppermute | solution.py:18
  69.8 8.2 %collective-permute-start.6 = (bf16[2,128,1024]{1,2,0:T(8,128)(2,1)}, bf16[2,128,1024]{1,2,0:T(8,128)(2,1)}, u32[]{:S(2)}, u32[]{:S(2)}) collective-permute-start(bf16[2,128,1024]{1,2,0:T(8,128)(2,1)} %collective-permute-done.5), channel_id=1, source_target_pairs={{0,1},{1,2},{2,3},{3,4},{4,5},{5,6},{6,7},{7,8},{8,9},{9,10},{10,1... | collective-permute-start | bytes 1572872 | tf_op jit(solution)/shard_map/ppermute | solution.py:18
  78.0 1.9 fusion.41
  80.9 1.9 fusion.42
  84.6 1.9 fusion.43
  88.3 4.4 %collective-permute-start.7 = (bf16[2,128,1024]{1,2,0:T(8,128)(2,1)}, bf16[2,128,1024]{1,2,0:T(8,128)(2,1)}, u32[]{:S(2)}, u32[]{:S(2)}) collective-permute-start(bf16[2,128,1024]{1,2,0:T(8,128)(2,1)} %collective-permute-done.6), channel_id=1, source_target_pairs={{0,1},{1,2},{2,3},{3,4},{4,5},{5,6},{6,7},{7,8},{8,9},{9,10},{10,1... | collective-permute-start | bytes 1572872 | tf_op jit(solution)/shard_map/ppermute | solution.py:18
  92.6 1.9 fusion.44
  96.3 1.9 fusion.45
  99.9 1.9 fusion.46
  103.6 1.9 fusion.47
  113.7 4.2 %fusion.6 = (bf16[8,128,1152]{1,2,0:T(8,128)(2,1)S(1)}, f32[8,1152,128]{2,1,0:T(8,128)}) fusion(pred[128,1152]{0,1:T(8,128)(4,1)S(1)} %compare_and_fusion, bf16[1152,8,128]{2,0,1:T(8,128)(2,1)S(1)} %constant_dynamic-update-slice_fusion.9, bf16[128,8,128]{0,2,1:T(8,128)(2,1)S(1)} %bitcast.120), kind=kOutput, calls=%fused_computation.27 | convolution fusion | flops 310247424 | bytes 9846784 | tf_op jit(solution)/shard_map/qhd,khd->hqk/dot_general | solution.py:34
  120.3 1.9 fusion.38
  123.4 4.8 %fusion.50 = f32[8,128,1152]{2,1,0:T(8,128)} fusion(bf16[128,8,128]{0,2,1:T(8,128)(2,1)S(1)} %bitcast.122, bf16[8,128,1152]{1,2,0:T(8,128)(2,1)} %copy-done.4), kind=kOutput, calls=%fused_computation.110 | convolution fusion | flops 301989888 | bytes 7340032 | tf_op jit(solution)/shard_map/hqk,qhd->khd/dot_general | solution.py:63
  128.3 2.8 fusion.9
  131.1 3.0 fusion.49
  134.1 6.0 %copy.63 = f32[1,1152,1024]{2,1,0:T(8,128)} copy(f32[1,1152,1024]{1,2,0:T(8,128)} %bitcast.115) | data formatting | bytes 9437184 | tf_op jit(solution)/shard_map/stack;reshape | solution.py:113
  140.2 6.1 %copy.64 = f32[1,1152,1024]{2,1,0:T(8,128)} copy(f32[1,1152,1024]{1,2,0:T(8,128)} %bitcast.114) | data formatting | bytes 9437184 | tf_op jit(solution)/shard_map/stack;reshape | solution.py:113
  149.3 5.8 %collective-permute-done.8 = f32[2,128,1024]{2,1,0:T(8,128)S(1)} collective-permute-done((f32[2,128,1024]{2,1,0:T(8,128)S(1)}, f32[2,128,1024]{2,1,0:T(8,128)S(1)}, u32[]{:S(2)}, u32[]{:S(2)}) %collective-permute-start.8) | collective-permute-done | bytes 1048608 | tf_op jit(solution)/shard_map/ppermute | solution.py:18
  158.8 3.6 fusion.31
  162.5 11.9 %collective-permute-done.9 = f32[2,128,1024]{2,1,0:T(8,128)} collective-permute-done((f32[2,128,1024]{2,1,0:T(8,128)}, f32[2,128,1024]{2,1,0:T(8,128)}, u32[]{:S(2)}, u32[]{:S(2)}) %collective-permute-start.9) | collective-permute-done | bytes 1048608 | tf_op jit(solution)/shard_map/ppermute | solution.py:18
  177.6 14.8 %collective-permute-done.10 = f32[2,128,1024]{2,1,0:T(8,128)S(1)} collective-permute-done((f32[2,128,1024]{2,1,0:T(8,128)S(1)}, f32[2,128,1024]{2,1,0:T(8,128)S(1)}, u32[]{:S(2)}, u32[]{:S(2)}) %collective-permute-start.10) | collective-permute-done | bytes 1048608 | tf_op jit(solution)/shard_map/ppermute | solution.py:18
  194.9 22.5 %collective-permute-done.11 = f32[2,128,1024]{2,1,0:T(8,128)S(1)} collective-permute-done((f32[2,128,1024]{2,1,0:T(8,128)S(1)}, f32[2,128,1024]{2,1,0:T(8,128)S(1)}, u32[]{:S(2)}, u32[]{:S(2)}) %collective-permute-start.11) | collective-permute-done | bytes 1048608 | tf_op jit(solution)/shard_map/ppermute | solution.py:18
  219.1 19.5 %collective-permute-done.12 = f32[2,128,1024]{2,1,0:T(8,128)S(1)} collective-permute-done((f32[2,128,1024]{2,1,0:T(8,128)S(1)}, f32[2,128,1024]{2,1,0:T(8,128)S(1)}, u32[]{:S(2)}, u32[]{:S(2)}) %collective-permute-start.12) | collective-permute-done | bytes 1048608 | tf_op jit(solution)/shard_map/ppermute | solution.py:18
  240.1 19.4 %collective-permute-done.13 = f32[2,128,1024]{2,1,0:T(8,128)S(1)} collective-permute-done((f32[2,128,1024]{2,1,0:T(8,128)S(1)}, f32[2,128,1024]{2,1,0:T(8,128)S(1)}, u32[]{:S(2)}, u32[]{:S(2)}) %collective-permute-start.13) | collective-permute-done | bytes 1048608 | tf_op jit(solution)/shard_map/ppermute | solution.py:18
  261.3 19.4 %collective-permute-done.14 = f32[2,128,1024]{2,1,0:T(8,128)S(1)} collective-permute-done((f32[2,128,1024]{2,1,0:T(8,128)S(1)}, f32[2,128,1024]{2,1,0:T(8,128)S(1)}, u32[]{:S(2)}, u32[]{:S(2)}) %collective-permute-start.14) | collective-permute-done | bytes 1048608 | tf_op jit(solution)/shard_map/ppermute | solution.py:18
  286.1 17.2 %collective-permute-done.15 = f32[2,128,1024]{2,1,0:T(8,128)} collective-permute-done((f32[2,128,1024]{2,1,0:T(8,128)}, f32[2,128,1024]{2,1,0:T(8,128)}, u32[]{:S(2)}, u32[]{:S(2)}) %collective-permute-start.15) | collective-permute-done | bytes 1048608 | tf_op jit(solution)/shard_map/ppermute | solution.py:18
  305.7 54.2 %reduce-scatter.2.cloned.1.call-done = f32[32,1024]{1,0:T(8,128)} async-done(((f32[1024,1024]{1,0:T(8,128)}), f32[32,1024]{1,0:T(8,128)}) %reduce-scatter.2.cloned.1.call-update) | async-done | bytes 131088 | tf_op jit(solution)/shard_map/reduce_scatter | solution.py:121
  (159 shorter events, 60.9 us)
Async XLA Ops:
  7.2 113.1 %copy-start = (bf16[1024,1024]{1,0:T(8,128)(2,1)S(1)}, bf16[1024,1024]{1,0:T(8,128)(2,1)}, u32[]{:S(2)}) copy-start(bf16[1024,1024]{1,0:T(8,128)(2,1)} %param.13) | copy-start | bytes 6291460
  7.2 50.7 %copy-start.26 = (s32[1,4096]{1,0:T(1,128)S(1)}, s32[1,4096]{1,0:T(1,128)}, u32[]{:S(2)}) copy-start(s32[1,4096]{1,0:T(1,128)} %param.12) | copy-start | bytes 49156
  7.2 352.7 %reduce-scatter.2.cloned.1.call-start = ((), (), s32[]{:S(2)}) async-start(), calls=%async_computation.1 | async-start | bytes 4325376 | tf_op jit(solution)/shard_map/reduce_scatter | solution.py:121
  9.7 3.9 %collective-permute-start = (bf16[2,128,1024]{1,2,0:T(8,128)(2,1)S(1)}, bf16[2,128,1024]{1,2,0:T(8,128)(2,1)S(1)}, u32[]{:S(2)}, u32[]{:S(2)}) collective-permute-start(bf16[2,128,1024]{1,2,0:T(8,128)(2,1)S(1)} %pad_maximum_fusion.1), channel_id=1, source_target_pairs={{0,1},{1,2},{2,3},{3,4},{4,5},{5,6},{6,7},{7,8},{8,9},{9,10},{10,1... | collective-permute-start | bytes 1572872 | tf_op jit(solution)/shard_map/ppermute | solution.py:18
  13.6 9.1 %copy-start.25 = (bf16[2,128,1024]{1,2,0:T(8,128)(2,1)}, bf16[2,128,1024]{1,2,0:T(8,128)(2,1)S(1)}, u32[]{:S(2)}) copy-start(bf16[2,128,1024]{1,2,0:T(8,128)(2,1)S(1)} %collective-permute-done) | copy-start | bytes 1572868
  13.6 10.6 %collective-permute-start.1 = (bf16[2,128,1024]{1,2,0:T(8,128)(2,1)S(1)}, bf16[2,128,1024]{1,2,0:T(8,128)(2,1)S(1)}, u32[]{:S(2)}, u32[]{:S(2)}) collective-permute-start(bf16[2,128,1024]{1,2,0:T(8,128)(2,1)S(1)} %collective-permute-done), channel_id=1, source_target_pairs={{0,1},{1,2},{2,3},{3,4},{4,5},{5,6},{6,7},{7,8},{8,9},{9,10},{10,1... | collective-permute-start | bytes 1572872 | tf_op jit(solution)/shard_map/ppermute | solution.py:18
  25.0 10.5 %collective-permute-start.2 = (bf16[2,128,1024]{1,2,0:T(8,128)(2,1)S(1)}, bf16[2,128,1024]{1,2,0:T(8,128)(2,1)S(1)}, u32[]{:S(2)}, u32[]{:S(2)}) collective-permute-start(bf16[2,128,1024]{1,2,0:T(8,128)(2,1)S(1)} %collective-permute-done.1), channel_id=1, source_target_pairs={{0,1},{1,2},{2,3},{3,4},{4,5},{5,6},{6,7},{7,8},{8,9},{9,10},{10,1... | collective-permute-start | bytes 1572872 | tf_op jit(solution)/shard_map/ppermute | solution.py:18
  36.3 10.5 %collective-permute-start.3 = (bf16[2,128,1024]{1,2,0:T(8,128)(2,1)S(1)}, bf16[2,128,1024]{1,2,0:T(8,128)(2,1)S(1)}, u32[]{:S(2)}, u32[]{:S(2)}) collective-permute-start(bf16[2,128,1024]{1,2,0:T(8,128)(2,1)S(1)} %collective-permute-done.2), channel_id=1, source_target_pairs={{0,1},{1,2},{2,3},{3,4},{4,5},{5,6},{6,7},{7,8},{8,9},{9,10},{10,1... | collective-permute-start | bytes 1572872 | tf_op jit(solution)/shard_map/ppermute | solution.py:18
  46.8 20.3 %copy-start.24 = (bf16[2,128,1024]{1,2,0:T(8,128)(2,1)}, bf16[2,128,1024]{1,2,0:T(8,128)(2,1)S(1)}, u32[]{:S(2)}) copy-start(bf16[2,128,1024]{1,2,0:T(8,128)(2,1)S(1)} %collective-permute-done.3) | copy-start | bytes 1572868
  46.8 11.2 %collective-permute-start.4 = (bf16[2,128,1024]{1,2,0:T(8,128)(2,1)S(1)}, bf16[2,128,1024]{1,2,0:T(8,128)(2,1)}, u32[]{:S(2)}, u32[]{:S(2)}) collective-permute-start(bf16[2,128,1024]{1,2,0:T(8,128)(2,1)S(1)} %collective-permute-done.3), channel_id=1, source_target_pairs={{0,1},{1,2},{2,3},{3,4},{4,5},{5,6},{6,7},{7,8},{8,9},{9,10},{10,1... | collective-permute-start | bytes 1572872 | tf_op jit(solution)/shard_map/ppermute | solution.py:18
  57.9 55.8 %copy-start.11 = (bf16[1,128,1024]{1,2,0:T(8,128)(2,1)}, bf16[1,128,1024]{1,2,0:T(8,128)(2,1)S(1)}, u32[]{:S(2)}) copy-start(bf16[1,128,1024]{1,2,0:T(8,128)(2,1)S(1)} %copy.74) | copy-start | bytes 786436
  58.0 11.8 %collective-permute-start.5 = (bf16[2,128,1024]{1,2,0:T(8,128)(2,1)}, bf16[2,128,1024]{1,2,0:T(8,128)(2,1)}, u32[]{:S(2)}, u32[]{:S(2)}) collective-permute-start(bf16[2,128,1024]{1,2,0:T(8,128)(2,1)} %collective-permute-done.4), channel_id=1, source_target_pairs={{0,1},{1,2},{2,3},{3,4},{4,5},{5,6},{6,7},{7,8},{8,9},{9,10},{10,1... | collective-permute-start | bytes 1572872 | tf_op jit(solution)/shard_map/ppermute | solution.py:18
  69.8 18.5 %collective-permute-start.6 = (bf16[2,128,1024]{1,2,0:T(8,128)(2,1)}, bf16[2,128,1024]{1,2,0:T(8,128)(2,1)}, u32[]{:S(2)}, u32[]{:S(2)}) collective-permute-start(bf16[2,128,1024]{1,2,0:T(8,128)(2,1)} %collective-permute-done.5), channel_id=1, source_target_pairs={{0,1},{1,2},{2,3},{3,4},{4,5},{5,6},{6,7},{7,8},{8,9},{9,10},{10,1... | collective-permute-start | bytes 1572872 | tf_op jit(solution)/shard_map/ppermute | solution.py:18
  88.3 15.3 %collective-permute-start.7 = (bf16[2,128,1024]{1,2,0:T(8,128)(2,1)}, bf16[2,128,1024]{1,2,0:T(8,128)(2,1)}, u32[]{:S(2)}, u32[]{:S(2)}) collective-permute-start(bf16[2,128,1024]{1,2,0:T(8,128)(2,1)} %collective-permute-done.6), channel_id=1, source_target_pairs={{0,1},{1,2},{2,3},{3,4},{4,5},{5,6},{6,7},{7,8},{8,9},{9,10},{10,1... | collective-permute-start | bytes 1572872 | tf_op jit(solution)/shard_map/ppermute | solution.py:18
  140.2 15.0 %slice-start = ((s8[4718592]{0:T(1024)(128)(4,1)}), s8[524288]{0:T(1024)(128)(4,1)S(1)}, s32[]{:S(2)}) async-start(s8[4718592]{0:T(1024)(128)(4,1)} %bitcast.108), calls=%async_computation.2 | async-start | bytes 1048576
  146.3 8.8 %copy-start.1 = (f32[1,1152,1024]{2,1,0:T(8,128)S(1)}, f32[1,1152,1024]{2,1,0:T(8,128)}, u32[]{:S(2)}) copy-start(f32[1,1152,1024]{2,1,0:T(8,128)} %copy.64) | copy-start | bytes 14155780
  147.8 9.9 %copy-start.29 = (f32[128]{0:T(128)S(1)}, f32[128]{0:T(128)}, u32[]{:S(2)}) copy-start(f32[128]{0:T(128)} %copy-done.27) | copy-start | bytes 1540
  147.8 9.9 %copy-start.31 = (f32[128]{0:T(128)S(1)}, f32[128]{0:T(128)}, u32[]{:S(2)}) copy-start(f32[128]{0:T(128)} %add_rsqrt_fusion) | copy-start | bytes 1540
  147.8 7.3 %collective-permute-start.8 = (f32[2,128,1024]{2,1,0:T(8,128)S(1)}, f32[2,128,1024]{2,1,0:T(8,128)S(1)}, u32[]{:S(2)}, u32[]{:S(2)}) collective-permute-start(f32[2,128,1024]{2,1,0:T(8,128)S(1)} %fusion.13), channel_id=1, source_target_pairs={{1,0},{2,1},{3,2},{4,3},{5,4},{6,5},{7,6},{8,7},{9,8},{10,9},{11,1... | collective-permute-start | bytes 3145736 | tf_op jit(solution)/shard_map/ppermute | solution.py:18
  156.2 18.1 %collective-permute-start.9 = (f32[2,128,1024]{2,1,0:T(8,128)}, f32[2,128,1024]{2,1,0:T(8,128)}, u32[]{:S(2)}, u32[]{:S(2)}) collective-permute-start(f32[2,128,1024]{2,1,0:T(8,128)} %fusion.15), channel_id=1, source_target_pairs={{1,0},{2,1},{3,2},{4,3},{5,4},{6,5},{7,6},{8,7},{9,8},{10,9},{11,1... | collective-permute-start | bytes 3145736 | tf_op jit(solution)/shard_map/ppermute | solution.py:18
  162.4 29.9 %slice-start.2 = ((s8[4718592]{0:T(1024)(128)(4,1)}), s8[524288]{0:T(1024)(128)(4,1)S(1)}, s32[]{:S(2)}) async-start(s8[4718592]{0:T(1024)(128)(4,1)} %bitcast.110), calls=%async_computation.4 | async-start | bytes 1048576
  162.4 29.9 %slice-start.3 = ((s8[4718592]{0:T(1024)(128)(4,1)}), s8[4194304]{0:T(1024)(128)(4,1)S(1)}, s32[]{:S(2)}) async-start(s8[4718592]{0:T(1024)(128)(4,1)} %bitcast.110), calls=%async_computation.5 | async-start | bytes 8388608
  174.3 43.1 %slice-start.4 = ((s8[4718592]{0:T(1024)(128)(4,1)}), s8[4194304]{0:T(1024)(128)(4,1)S(1)}, s32[]{:S(2)}) async-start(s8[4718592]{0:T(1024)(128)(4,1)} %bitcast.112), calls=%async_computation.6 | async-start | bytes 8388608
  176.1 41.3 %slice-start.5 = ((s8[4718592]{0:T(1024)(128)(4,1)}), s8[524288]{0:T(1024)(128)(4,1)S(1)}, s32[]{:S(2)}) async-start(s8[4718592]{0:T(1024)(128)(4,1)} %bitcast.112), calls=%async_computation.7 | async-start | bytes 1048576
  176.1 16.2 %collective-permute-start.10 = (f32[2,128,1024]{2,1,0:T(8,128)S(1)}, f32[2,128,1024]{2,1,0:T(8,128)S(1)}, u32[]{:S(2)}, u32[]{:S(2)}) collective-permute-start(f32[2,128,1024]{2,1,0:T(8,128)S(1)} %fusion.17), channel_id=1, source_target_pairs={{1,0},{2,1},{3,2},{4,3},{5,4},{6,5},{7,6},{8,7},{9,8},{10,9},{11,1... | collective-permute-start | bytes 3145736 | tf_op jit(solution)/shard_map/ppermute | solution.py:18
  193.6 23.8 %collective-permute-start.11 = (f32[2,128,1024]{2,1,0:T(8,128)S(1)}, f32[2,128,1024]{2,1,0:T(8,128)S(1)}, u32[]{:S(2)}, u32[]{:S(2)}) collective-permute-start(f32[2,128,1024]{2,1,0:T(8,128)S(1)} %fusion.19), channel_id=1, source_target_pairs={{1,0},{2,1},{3,2},{4,3},{5,4},{6,5},{7,6},{8,7},{9,8},{10,9},{11,1... | collective-permute-start | bytes 3145736 | tf_op jit(solution)/shard_map/ppermute | solution.py:18
  217.6 21.0 %collective-permute-start.12 = (f32[2,128,1024]{2,1,0:T(8,128)S(1)}, f32[2,128,1024]{2,1,0:T(8,128)S(1)}, u32[]{:S(2)}, u32[]{:S(2)}) collective-permute-start(f32[2,128,1024]{2,1,0:T(8,128)S(1)} %fusion.21), channel_id=1, source_target_pairs={{1,0},{2,1},{3,2},{4,3},{5,4},{6,5},{7,6},{8,7},{9,8},{10,9},{11,1... | collective-permute-start | bytes 3145736 | tf_op jit(solution)/shard_map/ppermute | solution.py:18
  238.8 20.7 %collective-permute-start.13 = (f32[2,128,1024]{2,1,0:T(8,128)S(1)}, f32[2,128,1024]{2,1,0:T(8,128)S(1)}, u32[]{:S(2)}, u32[]{:S(2)}) collective-permute-start(f32[2,128,1024]{2,1,0:T(8,128)S(1)} %fusion.23), channel_id=1, source_target_pairs={{1,0},{2,1},{3,2},{4,3},{5,4},{6,5},{7,6},{8,7},{9,8},{10,9},{11,1... | collective-permute-start | bytes 3145736 | tf_op jit(solution)/shard_map/ppermute | solution.py:18
  259.7 23.4 %copy-start.3 = (bf16[8,128,1152]{1,2,0:T(8,128)(2,1)S(1)}, bf16[8,128,1152]{1,2,0:T(8,128)(2,1)}, u32[]{:S(2)}) copy-start(bf16[8,128,1152]{1,2,0:T(8,128)(2,1)} %copy-done.2) | copy-start | bytes 7077892
  259.7 23.4 %copy-start.8 = (bf16[1152,8,128]{2,0,1:T(8,128)(2,1)S(1)}, bf16[1152,8,128]{2,0,1:T(8,128)(2,1)}, u32[]{:S(2)}) copy-start(bf16[1152,8,128]{2,0,1:T(8,128)(2,1)} %copy-done.7) | copy-start | bytes 7077892
  259.7 21.0 %collective-permute-start.14 = (f32[2,128,1024]{2,1,0:T(8,128)S(1)}, f32[2,128,1024]{2,1,0:T(8,128)S(1)}, u32[]{:S(2)}, u32[]{:S(2)}) collective-permute-start(f32[2,128,1024]{2,1,0:T(8,128)S(1)} %fusion.25), channel_id=1, source_target_pairs={{1,0},{2,1},{3,2},{4,3},{5,4},{6,5},{7,6},{8,7},{9,8},{10,9},{11,1... | collective-permute-start | bytes 3145736 | tf_op jit(solution)/shard_map/ppermute | solution.py:18
  281.8 21.4 %collective-permute-start.15 = (f32[2,128,1024]{2,1,0:T(8,128)}, f32[2,128,1024]{2,1,0:T(8,128)}, u32[]{:S(2)}, u32[]{:S(2)}) collective-permute-start(f32[2,128,1024]{2,1,0:T(8,128)} %fusion.12), channel_id=1, source_target_pairs={{1,0},{2,1},{3,2},{4,3},{5,4},{6,5},{7,6},{8,7},{9,8},{10,9},{11,1... | collective-permute-start | bytes 3145736 | tf_op jit(solution)/shard_map/ppermute | solution.py:18
  (24 other events, 81.9 us)
Sparse Core Ops, SparseCore 0:
  162.6 197.2 reduce-scatter.1
where the time goes:
time: 368 us; the launch traced here: 367 us
  waiting for transfers between devices  191 us (52%)
  starting transfers between devices  72.1 us (20%)
  local copies, waits for them, and re-layouts  53.6 us (15%)
  matrix products  23.2 us (6%)
  between operations  14.8 us (4%)
  other arithmetic  12.5 us (3%)
    ppermute x16, waiting for transfers between devices, from_behind(): return lax.ppermute(block, axis, route)  136 us
    ppermute x16, starting transfers between devices, from_behind(): return lax.ppermute(block, axis, route)  72 us
    reduce_scatter x1, waiting for transfers between devices, shards(): lax.psum_scatter(weight_part, ('dp', 'seq'), scatter_dimension=0, tiled=T...  54.2 us
    slice x8, local copies, waits for them, and re-layouts, shards(): key_rows = jnp.concatenate([block[0] for block in ordered])  14.8 us
    concatenate x10, local copies, waits for them, and re-layouts, shards(): key_rows = jnp.concatenate([block[0] for block in ordered])  12.3 us
    another operation x2, local copies, waits for them, and re-layouts, shards(): grads_all = jnp.stack([dkey_rows, dvalue_rows])  12.2 us
    unnamed x97, local copies, waits for them, and re-layouts  11.8 us
  transfers between devices with their start and end apart: 17, of which 13 were waited for; matrix products, arithmetic and copies ran while one was open for 11% of the time, Pallas kernels for 0%

commit v1 on v0

v1 whole, which is shorter than its diff:
```python
import functools
import math

import jax
import jax.numpy as jnp
from jax import lax
from jax.experimental import pallas as pl
from jax.experimental.pallas import tpu as pltpu
from jax.sharding import PartitionSpec as P

HEADS = 8
EPS = 1e-05
F32 = jnp.float32
BF16 = jnp.bfloat16


def dot_nn(a, b):
    return lax.dot_general(a, b, (((1,), (0,)), ((), ())), preferred_element_type=F32)


def dot_nt(a, b):
    return lax.dot_general(a, b, (((1,), (1,)), ((), ())), preferred_element_type=F32)


def dot_tn(a, b):
    return lax.dot_general(a, b, (((0,), (0,)), ((), ())), preferred_element_type=F32)


def kernel(
    groups,
    q_ref, k_ref, v_ref, gate_ref, cot_ref, w_ref, segrow_ref, segcol_ref,
    out_ref, dq_ref, dk_ref, dv_ref, dgate_ref, wpart_ref,
    qh, kh, vh, wts, slope, mix_stage, mix_in, dgated, gated, dmix_stage, dmh,
    dq_stage, dk_acc, dv_acc, dk_stage, dv_stage, dq_in, own_in, next_in,
    s_qkv, r_qkv, s_nxt, r_nxt, s_mix, r_mix, s_dm, r_dm, s_dq, r_dq, s_own, r_own, s_prv, r_prv,
):
    rows = q_ref.shape[0]
    features = q_ref.shape[1]
    hd = features // HEADS
    span = HEADS * rows
    win = span + rows
    scale = 1.0 / math.sqrt(hd)
    me = lax.axis_index("seq")
    g = me // HEADS
    p = lax.rem(me, HEADS)
    base = g * HEADS
    has_prev = g > 0
    has_next = g < groups - 1

    def rs(i):
        return pl.ds(pl.multiple_of(i * rows, rows), rows)

    def cs(i):
        return pl.ds(pl.multiple_of(i * hd, hd), hd)

    def peer(o):
        return lax.rem(p + o, HEADS)

    def source(o):
        return lax.rem(p + HEADS - o, HEADS)

    def copy(src, dst, ss, rsem, dev):
        return pltpu.make_async_remote_copy(
            src_ref=src, dst_ref=dst, send_sem=ss, recv_sem=rsem,
            device_id={"seq": dev}, device_id_type=pl.DeviceIdType.MESH,
        )

    barrier = pltpu.get_barrier_semaphore()

    def greet(dev):
        pl.semaphore_signal(
            barrier, inc=1, device_id={"seq": dev}, device_id_type=pl.DeviceIdType.MESH
        )

    for o in range(1, HEADS):
        greet(base + peer(o))

    @pl.when(has_next)
    def _():
        for o in range(HEADS):
            greet(base + HEADS + peer(o))

    @pl.when(has_prev)
    def _():
        for o in range(HEADS):
            greet(base - HEADS + peer(o))

    sides = jnp.minimum(g, 1) + jnp.minimum(groups - 1 - g, 1)
    pl.semaphore_wait(barrier, HEADS - 1 + HEADS * sides)

    ins = ((k_ref, kh, HEADS), (v_ref, vh, HEADS), (q_ref, qh, 0))

    def qkv_copy(kind, o, where):
        src, dst, off = ins[kind]
        return copy(src.at[:, cs(peer(o))], dst.at[rs(off + where)],
                    s_qkv.at[kind, o], r_qkv.at[kind, o], base + peer(o))

    def nxt_copy(kind, o, where):
        src, dst, _ = ins[kind]
        return copy(src.at[:, cs(peer(o))], dst.at[rs(where)],
                    s_nxt.at[kind, o], r_nxt.at[kind, o], base + HEADS + peer(o))

    @pl.when(has_next)
    def _():
        for kind in range(2):
            for o in range(HEADS):
                nxt_copy(kind, o, p).start()

    for kind in range(3):
        for o in range(1, HEADS):
            qkv_copy(kind, o, p).start()
    for src, dst, off in ins:
        dst[rs(off + p), :] = src[:, cs(p)]

    @pl.when(jnp.logical_not(has_prev))
    def _():
        kh[pl.ds(0, span), :] = jnp.zeros((span, hd), BF16)
        vh[pl.ds(0, span), :] = jnp.zeros((span, hd), BF16)

    dgated[...] = dot_nt(cot_ref[...], w_ref[...])
    dk_acc[...] = jnp.zeros_like(dk_acc)
    dv_acc[...] = jnp.zeros_like(dv_acc)

    for kind in range(3):
        for o in range(1, HEADS):
            qkv_copy(kind, o, source(o)).wait_recv()

    @pl.when(has_prev)
    def _():
        for kind in range(2):
            for o in range(HEADS):
                nxt_copy(kind, o, source(o)).wait_recv()

    def mix_copy(o, b, col):
        return copy(mix_stage.at[rs(b)], mix_in.at[:, cs(col)],
                    s_mix.at[o], r_mix.at[o], base + peer(o))

    def forward(i, carry):
        o = i + 1
        b = peer(o)
        win_rows = pl.ds(pl.multiple_of(b * rows, rows), win)
        scores = dot_nt(qh[rs(b), :], kh[win_rows, :]) * scale
        qi = lax.broadcasted_iota(jnp.int32, (rows, win), 0)
        kj = lax.broadcasted_iota(jnp.int32, (rows, win), 1)
        allowed = (segcol_ref[rs(b), :] == segrow_ref[:, win_rows]) & (kj - span <= qi)
        sig = 1.0 / (1.0 + jnp.exp(-scores))
        w = jnp.where(allowed, scores * sig, 0.0).astype(BF16)
        wts[rs(b), :] = w
        slope[rs(b), :] = jnp.where(
            allowed, (scale * sig) * (1.0 + scores * (1.0 - sig)), 0.0
        )
        mix_stage[rs(b), :] = dot_nn(w, vh[win_rows, :])

        @pl.when(o < HEADS)
        def _():
            mix_copy(o, b, p).start()

        return carry

    lax.fori_loop(0, HEADS, forward, 0)
    mix_in[:, cs(p)] = mix_stage[rs(p), :]
    for o in range(1, HEADS):
        mix_copy(o, p, source(o)).wait_recv()

    mixed = mix_in[...]
    centred = mixed - jnp.mean(mixed, axis=-1, keepdims=True)
    inverse = lax.rsqrt(jnp.mean(centred * centred, axis=-1, keepdims=True) + EPS)
    normed = centred * inverse
    gate = gate_ref[...].astype(F32)
    dg = dgated[...]
    dnormed = dg * gate
    dmixed = inverse * (
        dnormed
        - jnp.mean(dnormed, axis=-1, keepdims=True)
        - normed * jnp.mean(dnormed * normed, axis=-1, keepdims=True)
    )
    dmix_stage[...] = dmixed.astype(BF16)

    def dm_copy(o, where):
        return copy(dmix_stage.at[:, cs(peer(o))], dmh.at[rs(where)],
                    s_dm.at[o], r_dm.at[o], base + peer(o))

    for o in range(1, HEADS):
        dm_copy(o, p).start()
    dmh[rs(p), :] = dmix_stage[:, cs(p)]
    dgate_ref[...] = (dg * normed).astype(BF16)
    gated[...] = (normed * gate).astype(BF16)
    out_ref[...] = dot_nn(gated[...], w_ref[...]).astype(BF16)

    def weight_chunk(c, carry):
        wpart_ref[rs(c), :] = dot_tn(gated[:, cs(c)], cot_ref[...])
        return carry

    lax.fori_loop(0, HEADS, weight_chunk, 0)
    for o in range(1, HEADS):
        dm_copy(o, source(o)).wait_recv()

    grads = ((dk_acc, dk_stage), (dv_acc, dv_stage))

    def dq_copy(b, dev, col):
        return copy(dq_stage.at[rs(b)], dq_in.at[:, cs(col)], s_dq.at[b], r_dq.at[col], base + dev)

    def prv_copy(kind, b, col):
        return copy(grads[kind][1].at[rs(b)], next_in.at[kind, :, cs(col)],
                    s_prv.at[kind, b], r_prv.at[kind, col], base - HEADS + b)

    def own_copy(kind, b, dev, col):
        return copy(grads[kind][1].at[rs(HEADS + b)], own_in.at[kind, :, cs(col)],
                    s_own.at[kind, b], r_own.at[kind, col], base + dev)

    def backward(b, carry):
        win_rows = pl.ds(pl.multiple_of(b * rows, rows), win)
        dm = dmh[rs(b), :]
        ds = (dot_nt(dm, vh[win_rows, :]) * slope[rs(b), :]).astype(BF16)
        dq_stage[rs(b), :] = dot_nn(ds, kh[win_rows, :]).astype(BF16)

        @pl.when(b != p)
        def _():
            dq_copy(b, b, p).start()

        dk_acc[win_rows, :] += dot_tn(ds, qh[rs(b), :])
        dv_acc[win_rows, :] += dot_tn(wts[rs(b), :], dm)
        for acc, stage in grads:
            stage[rs(b), :] = acc[rs(b), :].astype(BF16)

        @pl.when(has_prev)
        def _():
            for kind in range(2):
                prv_copy(kind, b, p).start()

        return carry

    lax.fori_loop(0, HEADS, backward, 0)
    for acc, stage in grads:
        stage[pl.ds(span, span), :] = acc[pl.ds(span, span), :].astype(BF16)
    for kind in range(2):
        for o in range(1, HEADS):
            own_copy(kind, peer(o), peer(o), p).start()
        own_in[kind, :, cs(p)] = grads[kind][1][rs(HEADS + p), :]
    dq_in[:, cs(p)] = dq_stage[rs(p), :]

    @pl.when(jnp.logical_not(has_next))
    def _():
        next_in[...] = jnp.zeros_like(next_in)

    for o in range(1, HEADS):
        dq_copy(peer(o), peer(o), source(o)).wait_recv()
    dq_ref[...] = dq_in[...]

    @pl.when(has_next)
    def _():
        for kind in range(2):
            for o in range(HEADS):
                prv_copy(kind, peer(o), source(o)).wait_recv()

    for kind in range(2):
        for o in range(1, HEADS):
            own_copy(kind, peer(o), peer(o), source(o)).wait_recv()
    for kind, ref in ((0, dk_ref), (1, dv_ref)):
        ref[...] = (own_in[kind].astype(F32) + next_in[kind].astype(F32)).astype(BF16)

    @pl.when(has_next)
    def _():
        for kind in range(2):
            for o in range(HEADS):
                nxt_copy(kind, o, p).wait_send()

    @pl.when(has_prev)
    def _():
        for kind in range(2):
            for o in range(HEADS):
                prv_copy(kind, peer(o), p).wait_send()

    for o in range(1, HEADS):
        for kind in range(3):
            qkv_copy(kind, o, p).wait_send()
        mix_copy(o, peer(o), p).wait_send()
        dm_copy(o, p).wait_send()
        dq_copy(peer(o), peer(o), p).wait_send()
        for kind in range(2):
            own_copy(kind, peer(o), peer(o), p).wait_send()


def shards(queries, keys, values, gates, cotangent, segment, w_out):
    rows, features = queries.shape[1:]
    hd = features // HEADS
    span = HEADS * rows
    groups = lax.axis_size("seq") // HEADS
    g = lax.axis_index("seq") // HEADS
    padded = jnp.concatenate([jnp.full((span,), -1, jnp.int32), segment[0]])
    seg_win = lax.dynamic_slice_in_dim(padded, g * span, 2 * span)
    vm = pl.BlockSpec(memory_space=pltpu.VMEM)
    token = jax.ShapeDtypeStruct((rows, features), BF16)
    dma = pltpu.SemaphoreType.DMA
    results = pl.pallas_call(
        functools.partial(kernel, groups),
        out_shape=(token,) * 5 + (jax.ShapeDtypeStruct((features, features), F32),),
        in_specs=[vm] * 8,
        out_specs=(vm,) * 6,
        scratch_shapes=[
            pltpu.VMEM((span, hd), BF16),
            pltpu.VMEM((2 * span, hd), BF16),
            pltpu.VMEM((2 * span, hd), BF16),
            pltpu.VMEM((span, span + rows), BF16),
            pltpu.VMEM((span, span + rows), F32),
            pltpu.VMEM((span, hd), F32),
            pltpu.VMEM((rows, features), F32),
            pltpu.VMEM((rows, features), F32),
            pltpu.VMEM((rows, features), BF16),
            pltpu.VMEM((rows, features), BF16),
            pltpu.VMEM((span, hd), BF16),
            pltpu.VMEM((span, hd), BF16),
            pltpu.VMEM((2 * span, hd), F32),
            pltpu.VMEM((2 * span, hd), F32),
            pltpu.VMEM((2 * span, hd), BF16),
            pltpu.VMEM((2 * span, hd), BF16),
            pltpu.VMEM((rows, features), BF16),
            pltpu.VMEM((2, rows, features), BF16),
            pltpu.VMEM((2, rows, features), BF16),
            dma((3, HEADS)), dma((3, HEADS)),
            dma((2, HEADS)), dma((2, HEADS)),
            dma((HEADS,)), dma((HEADS,)),
            dma((HEADS,)), dma((HEADS,)),
            dma((HEADS,)), dma((HEADS,)),
            dma((2, HEADS)), dma((2, HEADS)),
            dma((2, HEADS)), dma((2, HEADS)),
        ],
        compiler_params=pltpu.CompilerParams(
            collective_id=0, has_side_effects=True, vmem_limit_bytes=48 * 1024 * 1024
        ),
        cost_estimate=pl.CostEstimate(
            flops=3_000_000_000, bytes_accessed=12_000_000, transcendentals=1_200_000
        ),
    )(
        queries[0], keys[0], values[0], gates[0], cotangent[0], w_out,
        seg_win[None], seg_win[span:, None],
    )
    output, dq, dk, dv, dgate, weight_part = results
    weight_grad = lax.psum_scatter(weight_part, ("dp", "seq"), scatter_dimension=0, tiled=True)
    return output[None], dq[None], dk[None], dv[None], dgate[None], weight_grad


def solution(mesh):
    tokens = P("dp", "seq", None)
    return jax.shard_map(
        shards,
        mesh=mesh,
        in_specs=(tokens,) * 5 + (P("dp", None), P()),
        out_specs=(tokens,) * 5 + (P(("dp", "seq"), None),),
        check_vma=False,
    )
```

time: 368 us -> 227 us (0.62)
  starting transfers between devices: 72.1 us -> 0.04 us
  Pallas kernels: 0 us -> 52 us
  local copies, waits for them, and re-layouts: 53.6 us -> 11.5 us
  waiting for transfers between devices: 191 us -> 149 us
  matrix products: 23.2 us -> 0 us
  other arithmetic: 12.5 us -> 0 us
    ppermute x16 -> x0, waiting for transfers between devices: 136 us -> none  [from_behind(): return lax.ppermute(block, axis, route)]
    reduce_scatter x1, waiting for transfers between devices: 54.2 us -> 149 us  [shards(): lax.psum_scatter(weight_part, ('dp', 'seq'), scatter_dimension=0, tiled=T...]
    ppermute x16 -> x0, starting transfers between devices: 72 us -> none  [from_behind(): return lax.ppermute(block, axis, route)]
    pallas_call x0 -> x1, Pallas kernels: none -> 52 us  [shards(): pl.pallas_call(functools.partial(kernel, groups), out_shape=(token,) * 5...]
    dot_general x9 -> x0, matrix products: 23.2 us -> none  [the longest x1 4.8 us: block_pass(): jnp.einsum('hqk,qhd->khd', weights, dmixed_heads, preferred_element_type=...]
    slice x9 -> x1, local copies, waits for them, and re-layouts: 15.6 us -> 0.69 us  [shards(): seg_win[span:, None]]
    another operation x3 -> x0, local copies, waits for them, and re-layouts: 13.3 us -> none  [the longest x2 12.2 us: shards(): grads_all = jnp.stack([dkey_rows, dvalue_rows])]
    concatenate x11 -> x0, local copies, waits for them, and re-layouts: 12.3 us -> none  [the longest x10 12.3 us: shards(): key_rows = jnp.concatenate([block[0] for block in ordered])]
  transfers between devices with their start and end apart: 17 -> 1, of which waited for: 13 -> 1; matrix products, arithmetic and copies ran while one was open for 11% -> 0% of each run, Pallas kernels for 0% -> 0%
where the time goes in v1:
time: 227 us; the launch traced here: 226 us
  waiting for transfers between devices  149 us (66%)
  Pallas kernels  52 us (23%)
  between operations  14.1 us (6%)
  local copies, waits for them, and re-layouts  11.5 us (5%)
    reduce_scatter x1, waiting for transfers between devices, shards(): lax.psum_scatter(weight_part, ('dp', 'seq'), scatter_dimension=0, tiled=T...  149 us
    pallas_call x1, Pallas kernels, shards(): pl.pallas_call(functools.partial(kernel, groups), out_shape=(token,) * 5...  52 us
    unnamed x17, local copies, waits for them, and re-layouts  9.85 us
  transfers between devices with their start and end apart: 1, of which 1 were waited for; matrix products, arithmetic and copies ran while one was open for 0% of the time, Pallas kernels for 0%

profile of v1, /device:TPU:0, one launch (start us, length us, event | category | flops | bytes accessed | tf_op | source)
XLA Modules:
  0.0 226.4 jit_solution(17684795608590148897)
XLA Ops:
  7.2 0.0 reduce-scatter.2.cloned.1.call-start
  7.2 0.7 pad_dynamic-slice_fusion.1
  7.9 0.7 pad_dynamic-slice_fusion
  8.6 0.2 copy.13.segcol_ref
  8.8 0.0 copy-start
  8.9 1.6 copy-done
  10.4 0.0 copy-start.1
  10.4 0.9 copy-done.1
  11.4 0.0 copy-start.2
  11.4 0.9 copy-done.2
  12.3 0.0 copy-start.3
  12.4 0.9 copy-done.3
  13.3 0.0 copy-start.4
  13.3 0.9 copy-done.4
  14.2 0.0 copy-start.5
  14.3 0.9 copy-done.5
  15.2 52.0 %shard_map.118 = (bf16[128,1024]{1,0:T(8,128)(2,1)S(1)}, bf16[128,1024]{1,0:T(8,128)(2,1)S(1)}, bf16[128,1024]{1,0:T(8,128)(2,1)S(1)}, bf16[128,1024]{1,0:T(8,12...) custom-call(bf16[128,1024]{1,0:T(8,128)(2,1)S(1)} %bitcast.19, bf16[128,1024]{1,0:T(8,128)(2,1)S(1)} %bitcast.20, ...), custom_call_target="tpu_custom_call" | custom-call | flops 3000000000 | bytes 12000000 | tf_op jit(solution)/shard_map/pallas_call | solution.py:295
  67.2 0.0 reduce-scatter.2.cloned.1.call-update
  67.2 148.8 %reduce-scatter.2.cloned.1.call-done = f32[32,1024]{1,0:T(8,128)} async-done(((f32[1024,1024]{1,0:T(8,128)}), f32[32,1024]{1,0:T(8,128)}) %reduce-scatter.2.cloned.1.call-update) | async-done | bytes 131088 | tf_op jit(solution)/shard_map/reduce_scatter | solution.py:339
  216.0 0.7 copy.19
  216.7 0.7 copy.20
  217.4 0.7 copy.21
  218.1 0.7 copy.22
  218.8 0.7 copy.23
Async XLA Ops:
  7.2 208.8 %reduce-scatter.2.cloned.1.call-start = ((), (), s32[]{:S(2)}) async-start(), calls=%async_computation.1 | async-start | bytes 4325376 | tf_op jit(solution)/shard_map/reduce_scatter | solution.py:339
  8.8 1.6 copy-start
  10.4 0.9 copy-start.1
  11.4 0.9 copy-start.2
  12.3 0.9 copy-start.3
  13.3 0.9 copy-start.4
  14.2 0.9 copy-start.5
Sparse Core Ops, SparseCore 0:
  67.4 148.6 reduce-scatter.1

commit v2 on v1

--- a/solution.py
+++ b/solution.py
@@ -27,12 +27,15 @@
 
 
 def kernel(
-    groups,
-    q_ref, k_ref, v_ref, gate_ref, cot_ref, w_ref, segrow_ref, segcol_ref,
-    out_ref, dq_ref, dk_ref, dv_ref, dgate_ref, wpart_ref,
+    groups, fused,
+    q_ref, k_ref, v_ref, gate_hbm, cot_hbm, w_hbm, seg_ref,
+    out_ref, dq_ref, dk_ref, dv_ref, dgate_ref, wgrad_ref,
+    gate_ref, cot_ref, w_ref, result, wresult, seg_win,
     qh, kh, vh, wts, slope, mix_stage, mix_in, dgated, gated, dmix_stage, dmh,
     dq_stage, dk_acc, dv_acc, dk_stage, dv_stage, dq_in, own_in, next_in,
+    part, part_send, pair_in, chip_acc, chip_send, chip_in, level_acc, level_send, level_in,
     s_qkv, r_qkv, s_nxt, r_nxt, s_mix, r_mix, s_dm, r_dm, s_dq, r_dq, s_own, r_own, s_prv, r_prv,
+    s_pair, r_pair, s_chip, r_chip, s_level, r_level, s_load, s_store,
 ):
     rows = q_ref.shape[0]
     features = q_ref.shape[1]
@@ -46,6 +49,9 @@
     base = g * HEADS
     has_prev = g > 0
     has_next = g < groups - 1
+    core = lax.rem(p, 2)
+    chip = p // 2
+    chips = HEADS // 2
 
     def rs(i):
         return pl.ds(pl.multiple_of(i * rows, rows), rows)
@@ -85,8 +91,36 @@
         for o in range(HEADS):
             greet(base - HEADS + peer(o))
 
+    def level(o):
+        return lax.rem(g + o, groups)
+
+    def level_source(o):
+        return lax.rem(g + groups - o, groups)
+
     sides = jnp.minimum(g, 1) + jnp.minimum(groups - 1 - g, 1)
-    pl.semaphore_wait(barrier, HEADS - 1 + HEADS * sides)
+    greeted = HEADS - 1 + HEADS * sides
+    if fused:
+        for o in range(1, groups):
+
+            @pl.when(jnp.abs(level(o) - g) > 1)
+            def _():
+                greet(level(o) * HEADS + p)
+
+        greeted = greeted + groups - 1 - sides
+    loads = [
+        pltpu.make_async_copy(src, dst, s_load.at[i])
+        for i, (src, dst) in enumerate(
+            (
+                (cot_hbm, cot_ref), (w_hbm, w_ref), (gate_hbm, gate_ref),
+                (k_ref.at[:, cs(p)], kh.at[rs(HEADS + p)]),
+                (v_ref.at[:, cs(p)], vh.at[rs(HEADS + p)]),
+                (q_ref.at[:, cs(p)], qh.at[rs(p)]),
+            )
+        )
+    ]
+    for load in loads:
+        load.start()
+    pl.semaphore_wait(barrier, greeted)
 
     ins = ((k_ref, kh, HEADS), (v_ref, vh, HEADS), (q_ref, qh, 0))
 
@@ -109,14 +143,18 @@
     for kind in range(3):
         for o in range(1, HEADS):
             qkv_copy(kind, o, p).start()
-    for src, dst, off in ins:
-        dst[rs(off + p), :] = src[:, cs(p)]
+    seg_own = seg_ref[:, pl.ds(pl.multiple_of(g * span, span), span)]
+    seg_before = seg_ref[:, pl.ds(pl.multiple_of(jnp.maximum(g - 1, 0) * span, span), span)]
+    seg_win[:, pl.ds(span, span)] = seg_own
+    seg_win[:, pl.ds(0, span)] = jnp.where(has_prev, seg_before, -1)
 
     @pl.when(jnp.logical_not(has_prev))
     def _():
         kh[pl.ds(0, span), :] = jnp.zeros((span, hd), BF16)
         vh[pl.ds(0, span), :] = jnp.zeros((span, hd), BF16)
 
+    for load in loads:
+        load.wait()
     dgated[...] = dot_nt(cot_ref[...], w_ref[...])
     dk_acc[...] = jnp.zeros_like(dk_acc)
     dv_acc[...] = jnp.zeros_like(dv_acc)
@@ -142,7 +180,9 @@
         scores = dot_nt(qh[rs(b), :], kh[win_rows, :]) * scale
         qi = lax.broadcasted_iota(jnp.int32, (rows, win), 0)
         kj = lax.broadcasted_iota(jnp.int32, (rows, win), 1)
-        allowed = (segcol_ref[rs(b), :] == segrow_ref[:, win_rows]) & (kj - span <= qi)
+        seg_q = seg_win[:, pl.ds(pl.multiple_of(span + b * rows, rows), rows)]
+        seg_q = jnp.transpose(jnp.broadcast_to(seg_q, (rows, rows)))[:, :1]
+        allowed = (seg_q == seg_win[:, win_rows]) & (kj - span <= qi)
         sig = 1.0 / (1.0 + jnp.exp(-scores))
         w = jnp.where(allowed, scores * sig, 0.0).astype(BF16)
         wts[rs(b), :] = w
@@ -183,15 +223,50 @@
     for o in range(1, HEADS):
         dm_copy(o, p).start()
     dmh[rs(p), :] = dmix_stage[:, cs(p)]
-    dgate_ref[...] = (dg * normed).astype(BF16)
     gated[...] = (normed * gate).astype(BF16)
-    out_ref[...] = dot_nn(gated[...], w_ref[...]).astype(BF16)
-
-    def weight_chunk(c, carry):
-        wpart_ref[rs(c), :] = dot_tn(gated[:, cs(c)], cot_ref[...])
-        return carry
-
-    lax.fori_loop(0, HEADS, weight_chunk, 0)
+    def chip_copy(o, where):
+        there = lax.rem(chip + o, chips)
+        return copy(chip_send.at[there], chip_in.at[where],
+                    s_chip.at[o], r_chip.at[o], base + 2 * there + core)
+
+    def level_copy(o, where):
+        return copy(level_send.at[level(o)], level_in.at[where],
+                    s_level.at[o], r_level.at[o], level(o) * HEADS + p)
+
+    if fused:
+        pair_copy = copy(part_send.at[1 - core], pair_in, s_pair, r_pair, base + p + 1 - 2 * core)
+        share = part.shape[3]
+        block = HEADS * share
+        for i in range(groups):
+            product = dot_tn(gated[:, i * block : (i + 1) * block], cot_ref[...])
+            for j in range(HEADS):
+                piece = product[j * share : (j + 1) * share]
+                part[j % 2, j // 2, i] = piece
+                part_send[j % 2, j // 2, i] = piece.astype(BF16)
+        pair_copy.start()
+    else:
+
+        def weight_chunk(c, carry):
+            wresult[rs(c), :] = dot_tn(gated[:, cs(c)], cot_ref[...])
+            return carry
+
+        lax.fori_loop(0, HEADS, weight_chunk, 0)
+    result[4] = (dg * normed).astype(BF16)
+    result[0] = dot_nn(gated[...], w_ref[...]).astype(BF16)
+    outs = (out_ref, dq_ref, dk_ref, dv_ref, dgate_ref)
+    stores = [
+        pltpu.make_async_copy(result.at[i], ref, s_store.at[i]) for i, ref in enumerate(outs)
+    ]
+    stores.append(pltpu.make_async_copy(wresult, wgrad_ref, s_store.at[5]))
+    stores[0].start()
+    stores[4].start()
+    if fused:
+        pair_copy.wait_recv()
+        for o in range(1, chips):
+            there = lax.rem(chip + o, chips)
+            chip_send[there] = (part[core, there] + pair_in[there].astype(F32)).astype(BF16)
+            chip_copy(o, chip).start()
+        chip_acc[...] = part[core, chip] + pair_in[chip].astype(F32)
     for o in range(1, HEADS):
         dm_copy(o, source(o)).wait_recv()
 
@@ -239,13 +314,25 @@
         own_in[kind, :, cs(p)] = grads[kind][1][rs(HEADS + p), :]
     dq_in[:, cs(p)] = dq_stage[rs(p), :]
 
+    if fused:
+        total = chip_acc[...]
+        for o in range(1, chips):
+            there = lax.rem(chip + chips - o, chips)
+            chip_copy(o, there).wait_recv()
+            total = total + chip_in[there].astype(F32)
+        level_acc[...] = total
+        level_send[...] = total.astype(BF16)
+        for o in range(1, groups):
+            level_copy(o, g).start()
+
     @pl.when(jnp.logical_not(has_next))
     def _():
         next_in[...] = jnp.zeros_like(next_in)
 
     for o in range(1, HEADS):
         dq_copy(peer(o), peer(o), source(o)).wait_recv()
-    dq_ref[...] = dq_in[...]
+    result[1] = dq_in[...]
+    stores[1].start()
 
     @pl.when(has_next)
     def _():
@@ -256,8 +343,16 @@
     for kind in range(2):
         for o in range(1, HEADS):
             own_copy(kind, peer(o), peer(o), source(o)).wait_recv()
-    for kind, ref in ((0, dk_ref), (1, dv_ref)):
-        ref[...] = (own_in[kind].astype(F32) + next_in[kind].astype(F32)).astype(BF16)
+    for kind in range(2):
+        result[2 + kind] = (own_in[kind].astype(F32) + next_in[kind].astype(F32)).astype(BF16)
+        stores[2 + kind].start()
+    if fused:
+        total = level_acc[g]
+        for o in range(1, groups):
+            level_copy(o, level_source(o)).wait_recv()
+            total = total + level_in[level_source(o)].astype(F32)
+        wresult[...] = total
+    stores[5].start()
 
     @pl.when(has_next)
     def _():
@@ -279,25 +374,44 @@
         dq_copy(peer(o), peer(o), p).wait_send()
         for kind in range(2):
             own_copy(kind, peer(o), peer(o), p).wait_send()
+    if fused:
+        pair_copy.wait_send()
+        for o in range(1, chips):
+            chip_copy(o, chip).wait_send()
+        for o in range(1, groups):
+            level_copy(o, g).wait_send()
+    for store in stores:
+        store.wait()
 
 
 def shards(queries, keys, values, gates, cotangent, segment, w_out):
     rows, features = queries.shape[1:]
     hd = features // HEADS
     span = HEADS * rows
+    chips = HEADS // 2
     groups = lax.axis_size("seq") // HEADS
     g = lax.axis_index("seq") // HEADS
-    padded = jnp.concatenate([jnp.full((span,), -1, jnp.int32), segment[0]])
-    seg_win = lax.dynamic_slice_in_dim(padded, g * span, 2 * span)
+    copies = lax.axis_size("dp") * groups * HEADS
+    share = features // copies
+    fused = lax.axis_size("dp") == 1 and share % 16 == 0
+    kept = share if fused else 16
+    wrows = share if fused else features
+    anywhere = pl.BlockSpec(memory_space=pl.ANY)
     vm = pl.BlockSpec(memory_space=pltpu.VMEM)
     token = jax.ShapeDtypeStruct((rows, features), BF16)
     dma = pltpu.SemaphoreType.DMA
     results = pl.pallas_call(
-        functools.partial(kernel, groups),
-        out_shape=(token,) * 5 + (jax.ShapeDtypeStruct((features, features), F32),),
-        in_specs=[vm] * 8,
-        out_specs=(vm,) * 6,
+        functools.partial(kernel, groups, fused),
+        out_shape=(token,) * 5 + (jax.ShapeDtypeStruct((wrows, features), F32),),
+        in_specs=[anywhere] * 6 + [vm],
+        out_specs=(anywhere,) * 6,
         scratch_shapes=[
+            pltpu.VMEM((rows, features), BF16),
+            pltpu.VMEM((rows, features), BF16),
+            pltpu.VMEM((features, features), BF16),
+            pltpu.VMEM((5, rows, features), BF16),
+            pltpu.VMEM((wrows, features), F32),
+            pltpu.VMEM((1, 2 * span), jnp.int32),
             pltpu.VMEM((span, hd), BF16),
             pltpu.VMEM((2 * span, hd), BF16),
             pltpu.VMEM((2 * span, hd), BF16),
@@ -317,6 +431,15 @@
             pltpu.VMEM((rows, features), BF16),
             pltpu.VMEM((2, rows, features), BF16),
             pltpu.VMEM((2, rows, features), BF16),
+            pltpu.VMEM((2, chips, groups, kept, features), F32),
+            pltpu.VMEM((2, chips, groups, kept, features), BF16),
+            pltpu.VMEM((chips, groups, kept, features), BF16),
+            pltpu.VMEM((groups, kept, features), F32),
+            pltpu.VMEM((chips, groups, kept, features), BF16),
+            pltpu.VMEM((chips, groups, kept, features), BF16),
+            pltpu.VMEM((groups, kept, features), F32),
+            pltpu.VMEM((groups, kept, features), BF16),
+            pltpu.VMEM((groups, kept, features), BF16),
             dma((3, HEADS)), dma((3, HEADS)),
             dma((2, HEADS)), dma((2, HEADS)),
             dma((HEADS,)), dma((HEADS,)),
@@ -324,6 +447,10 @@
             dma((HEADS,)), dma((HEADS,)),
             dma((2, HEADS)), dma((2, HEADS)),
             dma((2, HEADS)), dma((2, HEADS)),
+            dma, dma,
+            dma((chips,)), dma((chips,)),
+            dma((groups,)), dma((groups,)),
+            dma((6,)), dma((6,)),
         ],
         compiler_params=pltpu.CompilerParams(
             collective_id=0, has_side_effects=True, vmem_limit_bytes=48 * 1024 * 1024
@@ -332,11 +459,11 @@
             flops=3_000_000_000, bytes_accessed=12_000_000, transcendentals=1_200_000
         ),
     )(
-        queries[0], keys[0], values[0], gates[0], cotangent[0], w_out,
-        seg_win[None], seg_win[span:, None],
+        queries[0], keys[0], values[0], gates[0], cotangent[0], w_out, segment,
     )
-    output, dq, dk, dv, dgate, weight_part = results
-    weight_grad = lax.psum_scatter(weight_part, ("dp", "seq"), scatter_dimension=0, tiled=True)
+    output, dq, dk, dv, dgate, weight_grad = results
+    if not fused:
+        weight_grad = lax.psum_scatter(weight_grad, ("dp", "seq"), scatter_dimension=0, tiled=True)
     return output[None], dq[None], dk[None], dv[None], dgate[None], weight_grad
 
 

time: 227 us -> 77.3 us (0.34)
  the two profiles are of different devices: /device:TPU:0 before, /device:TPU:17 now
where the time goes in v2:
time: 77.3 us; the launch traced here: 77 us
  Pallas kernels  65.1 us (84%)
  local copies, waits for them, and re-layouts  11.2 us (14%)
    pallas_call x1, Pallas kernels, shards(): pl.pallas_call(functools.partial(kernel, groups, fused), out_shape=(token...  65.1 us
    unnamed x20, local copies, waits for them, and re-layouts  11.2 us

profile of v2, /device:TPU:17, one launch (start us, length us, event | category | flops | bytes accessed | tf_op | source)
XLA Modules:
  0.0 77.0 jit_solution(17969198601817901843)
XLA Ops:
  0.6 0.0 copy-start
  0.6 1.6 %copy-done = bf16[1024,1024]{1,0:T(8,128)(2,1)S(1)} copy-done((bf16[1024,1024]{1,0:T(8,128)(2,1)S(1)}, bf16[1024,1024]{1,0:T(8,128)(2,1)}, u32[]{:S(2)}) %copy-start) | copy-done | bytes 2097176
  2.2 0.0 copy-start.1
  2.2 0.9 %copy-done.1 = bf16[1,128,1024]{2,1,0:T(8,128)(2,1)S(1)} copy-done((bf16[1,128,1024]{2,1,0:T(8,128)(2,1)S(1)}, bf16[1,128,1024]{2,1,0:T(8,128)(2,1)}, u32[]{:S(2)}) %copy-start.1) | copy-done | bytes 262168
  3.2 0.0 copy-start.2
  3.2 0.9 %copy-done.2 = bf16[1,128,1024]{2,1,0:T(8,128)(2,1)S(1)} copy-done((bf16[1,128,1024]{2,1,0:T(8,128)(2,1)S(1)}, bf16[1,128,1024]{2,1,0:T(8,128)(2,1)}, u32[]{:S(2)}) %copy-start.2) | copy-done | bytes 262168
  4.1 0.0 copy-start.3
  4.1 0.9 %copy-done.3 = bf16[1,128,1024]{2,1,0:T(8,128)(2,1)S(1)} copy-done((bf16[1,128,1024]{2,1,0:T(8,128)(2,1)S(1)}, bf16[1,128,1024]{2,1,0:T(8,128)(2,1)}, u32[]{:S(2)}) %copy-start.3) | copy-done | bytes 262168
  5.1 0.0 copy-start.4
  5.1 0.9 %copy-done.4 = bf16[1,128,1024]{2,1,0:T(8,128)(2,1)S(1)} copy-done((bf16[1,128,1024]{2,1,0:T(8,128)(2,1)S(1)}, bf16[1,128,1024]{2,1,0:T(8,128)(2,1)}, u32[]{:S(2)}) %copy-start.4) | copy-done | bytes 262168
  6.0 0.0 copy-start.5
  6.0 0.9 %copy-done.5 = bf16[1,128,1024]{2,1,0:T(8,128)(2,1)S(1)} copy-done((bf16[1,128,1024]{2,1,0:T(8,128)(2,1)S(1)}, bf16[1,128,1024]{2,1,0:T(8,128)(2,1)}, u32[]{:S(2)}) %copy-start.5) | copy-done | bytes 262168
  7.0 0.0 copy-start.6
  7.0 0.7 copy-done.6
  7.7 65.1 %shard_map.118 = (bf16[128,1024]{1,0:T(8,128)(2,1)S(1)}, bf16[128,1024]{1,0:T(8,128)(2,1)S(1)}, bf16[128,1024]{1,0:T(8,128)(2,1)S(1)}, bf16[128,1024]{1,0:T(8,12...) custom-call(bf16[128,1024]{1,0:T(8,128)(2,1)S(1)} %bitcast.15, bf16[128,1024]{1,0:T(8,128)(2,1)S(1)} %bitcast.16, ...), custom_call_target="tpu_custom_call" | custom-call | flops 3000000000 | bytes 12000000 | tf_op jit(solution)/shard_map/pallas_call | solution.py:403
  72.8 0.7 copy.19
  73.5 0.7 copy.20
  74.2 0.7 copy.21
  74.9 0.7 copy.22
  75.6 0.7 copy.23
  76.3 0.7 copy.24
Async XLA Ops:
  0.6 1.6 %copy-start = (bf16[1024,1024]{1,0:T(8,128)(2,1)S(1)}, bf16[1024,1024]{1,0:T(8,128)(2,1)}, u32[]{:S(2)}) copy-start(bf16[1024,1024]{1,0:T(8,128)(2,1)} %w_hbm.1) | copy-start | bytes 6291460
  2.2 0.9 %copy-start.1 = (bf16[1,128,1024]{2,1,0:T(8,128)(2,1)S(1)}, bf16[1,128,1024]{2,1,0:T(8,128)(2,1)}, u32[]{:S(2)}) copy-start(bf16[1,128,1024]{2,1,0:T(8,128)(2,1)} %param.7) | copy-start | bytes 786436
  3.2 0.9 %copy-start.2 = (bf16[1,128,1024]{2,1,0:T(8,128)(2,1)S(1)}, bf16[1,128,1024]{2,1,0:T(8,128)(2,1)}, u32[]{:S(2)}) copy-start(bf16[1,128,1024]{2,1,0:T(8,128)(2,1)} %param.8) | copy-start | bytes 786436
  4.1 0.9 %copy-start.3 = (bf16[1,128,1024]{2,1,0:T(8,128)(2,1)S(1)}, bf16[1,128,1024]{2,1,0:T(8,128)(2,1)}, u32[]{:S(2)}) copy-start(bf16[1,128,1024]{2,1,0:T(8,128)(2,1)} %param.9) | copy-start | bytes 786436
  5.1 0.9 %copy-start.4 = (bf16[1,128,1024]{2,1,0:T(8,128)(2,1)S(1)}, bf16[1,128,1024]{2,1,0:T(8,128)(2,1)}, u32[]{:S(2)}) copy-start(bf16[1,128,1024]{2,1,0:T(8,128)(2,1)} %param.10) | copy-start | bytes 786436
  6.0 0.9 %copy-start.5 = (bf16[1,128,1024]{2,1,0:T(8,128)(2,1)S(1)}, bf16[1,128,1024]{2,1,0:T(8,128)(2,1)}, u32[]{:S(2)}) copy-start(bf16[1,128,1024]{2,1,0:T(8,128)(2,1)} %param.11) | copy-start | bytes 786436
  7.0 0.7 copy-start.6

commit v3 on v2

--- a/solution.py
+++ b/solution.py
@@ -30,9 +30,9 @@
     groups, fused,
     q_ref, k_ref, v_ref, gate_hbm, cot_hbm, w_hbm, seg_ref,
     out_ref, dq_ref, dk_ref, dv_ref, dgate_ref, wgrad_ref,
-    gate_ref, cot_ref, w_ref, result, wresult, seg_win,
-    qh, kh, vh, wts, slope, mix_stage, mix_in, dgated, gated, dmix_stage, dmh,
-    dq_stage, dk_acc, dv_acc, dk_stage, dv_stage, dq_in, own_in, next_in,
+    gate_ref, cot_ref, w_ref, result, wresult, seg_win, seg_col,
+    qh, kh, vh, k_turned, v_turned, wts, slope, mix_part, mix_stage, mix_in, dgated, gated,
+    dmix_stage, dmh, dq_part, dq_stage, dk_acc, dv_acc, dk_stage, dv_stage, dq_in, own_in, next_in,
     part, part_send, pair_in, chip_acc, chip_send, chip_in, level_acc, level_send, level_in,
     s_qkv, r_qkv, s_nxt, r_nxt, s_mix, r_mix, s_dm, r_dm, s_dq, r_dq, s_own, r_own, s_prv, r_prv,
     s_pair, r_pair, s_chip, r_chip, s_level, r_level, s_load, s_store,
@@ -41,7 +41,7 @@
     features = q_ref.shape[1]
     hd = features // HEADS
     span = HEADS * rows
-    win = span + rows
+    wide = 2 * rows
     scale = 1.0 / math.sqrt(hd)
     me = lax.axis_index("seq")
     g = me // HEADS
@@ -81,32 +81,14 @@
     for o in range(1, HEADS):
         greet(base + peer(o))
 
-    @pl.when(has_next)
-    def _():
-        for o in range(HEADS):
-            greet(base + HEADS + peer(o))
-
-    @pl.when(has_prev)
-    def _():
-        for o in range(HEADS):
-            greet(base - HEADS + peer(o))
-
     def level(o):
         return lax.rem(g + o, groups)
 
     def level_source(o):
         return lax.rem(g + groups - o, groups)
 
-    sides = jnp.minimum(g, 1) + jnp.minimum(groups - 1 - g, 1)
-    greeted = HEADS - 1 + HEADS * sides
-    if fused:
-        for o in range(1, groups):
-
-            @pl.when(jnp.abs(level(o) - g) > 1)
-            def _():
-                greet(level(o) * HEADS + p)
-
-        greeted = greeted + groups - 1 - sides
+    for o in range(1, groups):
+        greet(level(o) * HEADS + p)
     loads = [
         pltpu.make_async_copy(src, dst, s_load.at[i])
         for i, (src, dst) in enumerate(
@@ -120,7 +102,7 @@
     ]
     for load in loads:
         load.start()
-    pl.semaphore_wait(barrier, greeted)
+    pl.semaphore_wait(barrier, HEADS + groups - 2)
 
     ins = ((k_ref, kh, HEADS), (v_ref, vh, HEADS), (q_ref, qh, 0))
 
@@ -129,20 +111,23 @@
         return copy(src.at[:, cs(peer(o))], dst.at[rs(off + where)],
                     s_qkv.at[kind, o], r_qkv.at[kind, o], base + peer(o))
 
-    def nxt_copy(kind, o, where):
-        src, dst, _ = ins[kind]
-        return copy(src.at[:, cs(peer(o))], dst.at[rs(where)],
-                    s_nxt.at[kind, o], r_nxt.at[kind, o], base + HEADS + peer(o))
+    def nxt_copy(kind, o):
+        src, dst, off = ins[kind]
+        at = source(o)
+        held = src.at[:, cs(p)] if o == 0 else dst.at[rs(off + at)]
+        return copy(held, dst.at[rs(at)], s_nxt.at[kind, at], r_nxt.at[kind, at],
+                    base + HEADS + p)
 
     @pl.when(has_next)
     def _():
         for kind in range(2):
-            for o in range(HEADS):
-                nxt_copy(kind, o, p).start()
-
-    for kind in range(3):
-        for o in range(1, HEADS):
+            nxt_copy(kind, 0).start()
+
+    for o in range(1, HEADS):
+        for kind in range(2):
             qkv_copy(kind, o, p).start()
+    for o in range(1, HEADS):
+        qkv_copy(2, o, p).start()
     seg_own = seg_ref[:, pl.ds(pl.multiple_of(g * span, span), span)]
     seg_before = seg_ref[:, pl.ds(pl.multiple_of(jnp.maximum(g - 1, 0) * span, span), span)]
     seg_win[:, pl.ds(span, span)] = seg_own
@@ -153,54 +138,89 @@
         kh[pl.ds(0, span), :] = jnp.zeros((span, hd), BF16)
         vh[pl.ds(0, span), :] = jnp.zeros((span, hd), BF16)
 
+    def seg_block(j, carry):
+        line = seg_win[:, rs(j)]
+        seg_col[rs(j), :] = jnp.transpose(jnp.broadcast_to(line, (rows, rows)))
+        return carry
+
+    lax.fori_loop(0, 2 * HEADS, seg_block, 0)
+    dk_acc[...] = jnp.zeros_like(dk_acc)
+    dv_acc[...] = jnp.zeros_like(dv_acc)
+    for o in range(1, HEADS):
+        for kind in range(2):
+            qkv_copy(kind, o, source(o)).wait_recv()
+
+            @pl.when(has_next)
+            def _():
+                nxt_copy(kind, o).start()
+
     for load in loads:
         load.wait()
     dgated[...] = dot_nt(cot_ref[...], w_ref[...])
-    dk_acc[...] = jnp.zeros_like(dk_acc)
-    dv_acc[...] = jnp.zeros_like(dv_acc)
-
-    for kind in range(3):
-        for o in range(1, HEADS):
-            qkv_copy(kind, o, source(o)).wait_recv()
+    for ref, turned in ((kh, k_turned), (vh, v_turned)):
+        turned[:, pl.ds(span, span)] = jnp.transpose(ref[pl.ds(span, span), :])
+    for o in range(1, HEADS):
+        qkv_copy(2, o, source(o)).wait_recv()
+
+    def bounds(i, own):
+        lo = span if own else i * wide
+        hi = span + (i + 1) * wide if own else span
+        return lo, hi, slice(lo - i * wide, hi - i * wide), slice(i * wide, (i + 1) * wide)
+
+    def forward(i, own):
+        lo, hi, held, mine = bounds(i, own)
+        scores = dot_nt(kh[lo:hi, :], qh[mine, :]) * scale
+        seg_k = seg_col[lo:hi, :]
+        seg_q = seg_win[:, span + i * wide : span + (i + 1) * wide]
+        allowed = jnp.concatenate([seg_k, seg_k], axis=1) == seg_q
+        if own:
+            kj = lax.broadcasted_iota(jnp.int32, scores.shape, 0)
+            qi = lax.broadcasted_iota(jnp.int32, scores.shape, 1)
+            allowed = allowed & (kj - i * wide <= qi)
+        sig = 1.0 / (1.0 + jnp.exp(-jnp.maximum(scores, -80.0)))
+        sig = jnp.where(allowed, sig, 0.0)
+        silu = scores * sig
+        w = silu.astype(BF16)
+        wts[i, held, :] = w
+        slope[i, held, :] = (sig + silu * (1.0 - sig)) * scale
+        return dot_nn(v_turned[:, lo:hi], w)
+
+    def mix_copy(t, dev, col):
+        return copy(mix_stage.at[rs(t)], mix_in.at[:, cs(col)],
+                    s_mix.at[t], r_mix.at[col], base + dev)
+
+    for i in range(chips):
+        mix_part[i] = forward(i, True)
 
     @pl.when(has_prev)
     def _():
-        for kind in range(2):
-            for o in range(HEADS):
-                nxt_copy(kind, o, source(o)).wait_recv()
-
-    def mix_copy(o, b, col):
-        return copy(mix_stage.at[rs(b)], mix_in.at[:, cs(col)],
-                    s_mix.at[o], r_mix.at[o], base + peer(o))
-
-    def forward(i, carry):
-        o = i + 1
-        b = peer(o)
-        win_rows = pl.ds(pl.multiple_of(b * rows, rows), win)
-        scores = dot_nt(qh[rs(b), :], kh[win_rows, :]) * scale
-        qi = lax.broadcasted_iota(jnp.int32, (rows, win), 0)
-        kj = lax.broadcasted_iota(jnp.int32, (rows, win), 1)
-        seg_q = seg_win[:, pl.ds(pl.multiple_of(span + b * rows, rows), rows)]
-        seg_q = jnp.transpose(jnp.broadcast_to(seg_q, (rows, rows)))[:, :1]
-        allowed = (seg_q == seg_win[:, win_rows]) & (kj - span <= qi)
-        sig = 1.0 / (1.0 + jnp.exp(-scores))
-        w = jnp.where(allowed, scores * sig, 0.0).astype(BF16)
-        wts[rs(b), :] = w
-        slope[rs(b), :] = jnp.where(
-            allowed, (scale * sig) * (1.0 + scores * (1.0 - sig)), 0.0
-        )
-        mix_stage[rs(b), :] = dot_nn(w, vh[win_rows, :])
-
-        @pl.when(o < HEADS)
-        def _():
-            mix_copy(o, b, p).start()
+        for o in range(HEADS):
+            for kind in range(2):
+                nxt_copy(kind, o).wait_recv()
+
+    for ref, turned in ((kh, k_turned), (vh, v_turned)):
+        turned[:, pl.ds(0, span)] = jnp.transpose(ref[pl.ds(0, span), :])
+
+    def finish(o, carry):
+        now = lax.rem(chip + 1 + o, chips)
+        for i in range(chips):
+
+            @pl.when(now == i)
+            def _():
+                mixed = mix_part[i] + forward(i, False)
+                mix_stage[i * wide : (i + 1) * wide, :] = jnp.transpose(mixed)
+                for t in (2 * i, 2 * i + 1):
+
+                    @pl.when(t != p)
+                    def _():
+                        mix_copy(t, t, p).start()
 
         return carry
 
-    lax.fori_loop(0, HEADS, forward, 0)
+    lax.fori_loop(0, chips, finish, 0)
     mix_in[:, cs(p)] = mix_stage[rs(p), :]
     for o in range(1, HEADS):
-        mix_copy(o, p, source(o)).wait_recv()
+        mix_copy(p, p, source(o)).wait_recv()
 
     mixed = mix_in[...]
     centred = mixed - jnp.mean(mixed, axis=-1, keepdims=True)
@@ -251,11 +271,13 @@
             return carry
 
         lax.fori_loop(0, HEADS, weight_chunk, 0)
-    result[4] = (dg * normed).astype(BF16)
+    result[1] = (dg * normed).astype(BF16)
     result[0] = dot_nn(gated[...], w_ref[...]).astype(BF16)
     outs = (out_ref, dq_ref, dk_ref, dv_ref, dgate_ref)
+    ready = (result.at[0], dq_in, own_in.at[0], own_in.at[1], result.at[1])
     stores = [
-        pltpu.make_async_copy(result.at[i], ref, s_store.at[i]) for i, ref in enumerate(outs)
+        pltpu.make_async_copy(src, ref, s_store.at[i])
+        for i, (src, ref) in enumerate(zip(ready, outs))
     ]
     stores.append(pltpu.make_async_copy(wresult, wgrad_ref, s_store.at[5]))
     stores[0].start()
@@ -275,45 +297,59 @@
     def dq_copy(b, dev, col):
         return copy(dq_stage.at[rs(b)], dq_in.at[:, cs(col)], s_dq.at[b], r_dq.at[col], base + dev)
 
-    def prv_copy(kind, b, col):
-        return copy(grads[kind][1].at[rs(b)], next_in.at[kind, :, cs(col)],
-                    s_prv.at[kind, b], r_prv.at[kind, col], base - HEADS + b)
+    def prv_copy(kind, i):
+        held = pl.ds(i * wide, wide)
+        return copy(grads[kind][1].at[held], next_in.at[kind, held],
+                    s_prv.at[kind, i], r_prv.at[kind, i], base - HEADS + p)
 
     def own_copy(kind, b, dev, col):
         return copy(grads[kind][1].at[rs(HEADS + b)], own_in.at[kind, :, cs(col)],
                     s_own.at[kind, b], r_own.at[kind, col], base + dev)
 
-    def backward(b, carry):
-        win_rows = pl.ds(pl.multiple_of(b * rows, rows), win)
-        dm = dmh[rs(b), :]
-        ds = (dot_nt(dm, vh[win_rows, :]) * slope[rs(b), :]).astype(BF16)
-        dq_stage[rs(b), :] = dot_nn(ds, kh[win_rows, :]).astype(BF16)
-
-        @pl.when(b != p)
-        def _():
-            dq_copy(b, b, p).start()
-
-        dk_acc[win_rows, :] += dot_tn(ds, qh[rs(b), :])
-        dv_acc[win_rows, :] += dot_tn(wts[rs(b), :], dm)
+    def backward(i, own):
+        lo, hi, held, mine = bounds(i, own)
+        dm = dmh[mine, :]
+        ds = (dot_nt(vh[lo:hi, :], dm) * slope[i, held, :]).astype(BF16)
+        dk_acc[lo:hi, :] += dot_nn(ds, qh[mine, :])
+        dv_acc[lo:hi, :] += dot_nn(wts[i, held, :], dm)
+        return dot_nn(k_turned[:, lo:hi], ds)
+
+    for i in range(chips):
+        dq_part[i] = backward(i, False)
+        held = pl.ds(i * wide, wide)
         for acc, stage in grads:
-            stage[rs(b), :] = acc[rs(b), :].astype(BF16)
+            stage[held, :] = acc[held, :].astype(BF16)
 
         @pl.when(has_prev)
         def _():
             for kind in range(2):
-                prv_copy(kind, b, p).start()
-
-        return carry
-
-    lax.fori_loop(0, HEADS, backward, 0)
-    for acc, stage in grads:
-        stage[pl.ds(span, span), :] = acc[pl.ds(span, span), :].astype(BF16)
+                prv_copy(kind, i).start()
+
+    for i in range(chips):
+        dq = dq_part[i] + backward(i, True)
+        dq_stage[i * wide : (i + 1) * wide, :] = jnp.transpose(dq).astype(BF16)
+    for o in range(1, HEADS):
+        dq_copy(peer(o), peer(o), p).start()
+    dq_in[:, cs(p)] = dq_stage[rs(p), :]
+
+    @pl.when(jnp.logical_not(has_next))
+    def _():
+        next_in[...] = jnp.zeros_like(next_in)
+
+    @pl.when(has_next)
+    def _():
+        for i in range(chips):
+            for kind in range(2):
+                prv_copy(kind, i).wait_recv()
+
+    for kind, (acc, stage) in enumerate(grads):
+        both = acc[pl.ds(span, span), :] + next_in[kind].astype(F32)
+        stage[pl.ds(span, span), :] = both.astype(BF16)
+    for o in range(1, HEADS):
+        for kind in range(2):
+            own_copy(kind, peer(o), peer(o), p).start()
     for kind in range(2):
-        for o in range(1, HEADS):
-            own_copy(kind, peer(o), peer(o), p).start()
         own_in[kind, :, cs(p)] = grads[kind][1][rs(HEADS + p), :]
-    dq_in[:, cs(p)] = dq_stage[rs(p), :]
-
     if fused:
         total = chip_acc[...]
         for o in range(1, chips):
@@ -325,26 +361,14 @@
         for o in range(1, groups):
             level_copy(o, g).start()
 
-    @pl.when(jnp.logical_not(has_next))
-    def _():
-        next_in[...] = jnp.zeros_like(next_in)
-
     for o in range(1, HEADS):
         dq_copy(peer(o), peer(o), source(o)).wait_recv()
-    result[1] = dq_in[...]
     stores[1].start()
-
-    @pl.when(has_next)
-    def _():
-        for kind in range(2):
-            for o in range(HEADS):
-                prv_copy(kind, peer(o), source(o)).wait_recv()
 
     for kind in range(2):
         for o in range(1, HEADS):
             own_copy(kind, peer(o), peer(o), source(o)).wait_recv()
     for kind in range(2):
-        result[2 + kind] = (own_in[kind].astype(F32) + next_in[kind].astype(F32)).astype(BF16)
         stores[2 + kind].start()
     if fused:
         total = level_acc[g]
@@ -358,18 +382,18 @@
     def _():
         for kind in range(2):
             for o in range(HEADS):
-                nxt_copy(kind, o, p).wait_send()
+                nxt_copy(kind, o).wait_send()
 
     @pl.when(has_prev)
     def _():
         for kind in range(2):
-            for o in range(HEADS):
-                prv_copy(kind, peer(o), p).wait_send()
+            for i in range(chips):
+                prv_copy(kind, i).wait_send()
 
     for o in range(1, HEADS):
         for kind in range(3):
             qkv_copy(kind, o, p).wait_send()
-        mix_copy(o, peer(o), p).wait_send()
+        mix_copy(peer(o), peer(o), p).wait_send()
         dm_copy(o, p).wait_send()
         dq_copy(peer(o), peer(o), p).wait_send()
         for kind in range(2):
@@ -409,20 +433,25 @@
             pltpu.VMEM((rows, features), BF16),
             pltpu.VMEM((rows, features), BF16),
             pltpu.VMEM((features, features), BF16),
-            pltpu.VMEM((5, rows, features), BF16),
+            pltpu.VMEM((2, rows, features), BF16),
             pltpu.VMEM((wrows, features), F32),
             pltpu.VMEM((1, 2 * span), jnp.int32),
+            pltpu.VMEM((2 * span, rows), jnp.int32),
             pltpu.VMEM((span, hd), BF16),
             pltpu.VMEM((2 * span, hd), BF16),
             pltpu.VMEM((2 * span, hd), BF16),
-            pltpu.VMEM((span, span + rows), BF16),
-            pltpu.VMEM((span, span + rows), F32),
+            pltpu.VMEM((hd, 2 * span), BF16),
+            pltpu.VMEM((hd, 2 * span), BF16),
+            pltpu.VMEM((chips, span + 2 * rows, 2 * rows), BF16),
+            pltpu.VMEM((chips, span + 2 * rows, 2 * rows), F32),
+            pltpu.VMEM((chips, hd, 2 * rows), F32),
             pltpu.VMEM((span, hd), F32),
             pltpu.VMEM((rows, features), F32),
             pltpu.VMEM((rows, features), F32),
             pltpu.VMEM((rows, features), BF16),
             pltpu.VMEM((rows, features), BF16),
             pltpu.VMEM((span, hd), BF16),
+            pltpu.VMEM((chips, hd, 2 * rows), F32),
             pltpu.VMEM((span, hd), BF16),
             pltpu.VMEM((2 * span, hd), F32),
             pltpu.VMEM((2 * span, hd), F32),
@@ -430,7 +459,7 @@
             pltpu.VMEM((2 * span, hd), BF16),
             pltpu.VMEM((rows, features), BF16),
             pltpu.VMEM((2, rows, features), BF16),
-            pltpu.VMEM((2, rows, features), BF16),
+            pltpu.VMEM((2, span, hd), BF16),
             pltpu.VMEM((2, chips, groups, kept, features), F32),
             pltpu.VMEM((2, chips, groups, kept, features), BF16),
             pltpu.VMEM((chips, groups, kept, features), BF16),
@@ -446,14 +475,14 @@
             dma((HEADS,)), dma((HEADS,)),
             dma((HEADS,)), dma((HEADS,)),
             dma((2, HEADS)), dma((2, HEADS)),
-            dma((2, HEADS)), dma((2, HEADS)),
+            dma((2, chips)), dma((2, chips)),
             dma, dma,
             dma((chips,)), dma((chips,)),
             dma((groups,)), dma((groups,)),
             dma((6,)), dma((6,)),
         ],
         compiler_params=pltpu.CompilerParams(
-            collective_id=0, has_side_effects=True, vmem_limit_bytes=48 * 1024 * 1024
+            collective_id=0, has_side_effects=True, vmem_limit_bytes=62 * 1024 * 1024
         ),
         cost_estimate=pl.CostEstimate(
             flops=3_000_000_000, bytes_accessed=12_000_000, transcendentals=1_200_000

time: 77.3 us -> 67.5 us (0.87)
  the two profiles are of different devices: /device:TPU:17 before, /device:TPU:0 now
where the time goes in v3:
time: 67.5 us; the launch traced here: 67 us
  Pallas kernels  58.2 us (86%)
  local copies, waits for them, and re-layouts  8.09 us (12%)
    pallas_call x1, Pallas kernels, shards(): pl.pallas_call(functools.partial(kernel, groups, fused), out_shape=(token...  58.2 us
    unnamed x10, local copies, waits for them, and re-layouts  8.09 us

profile of v3, /device:TPU:0, one launch (start us, length us, event | category | flops | bytes accessed | tf_op | source)
XLA Modules:
  0.0 67.0 jit_solution(166539494682074856)
XLA Ops:
  0.6 58.2 %shard_map.118 = (bf16[128,1024]{1,0:T(8,128)(2,1)}, bf16[128,1024]{1,0:T(8,128)(2,1)}, bf16[128,1024]{1,0:T(8,128)(2,1)}, bf16[128,1024]{1,0:T(8,128)(2,1)}, bf...) custom-call(bf16[128,1024]{1,0:T(8,128)(2,1)} %bitcast.15, bf16[128,1024]{1,0:T(8,128)(2,1)} %bitcast.16, ...), custom_call_target="tpu_custom_call" | custom-call | flops 3000000000 | bytes 12000000 | tf_op jit(solution)/shard_map/pallas_call | solution.py:427
  58.9 0.0 copy-start
  58.9 0.0 copy-start.1
  58.9 1.7 %copy.19 = bf16[1,128,1024]{2,1,0:T(8,128)(2,1)} copy(bf16[1,128,1024]{2,1,0:T(8,128)(2,1)} %bitcast.14) | data formatting | bytes 524288
  60.6 1.7 %copy.20 = bf16[1,128,1024]{2,1,0:T(8,128)(2,1)} copy(bf16[1,128,1024]{2,1,0:T(8,128)(2,1)} %bitcast.13) | data formatting | bytes 524288
  62.3 1.7 %copy.21 = bf16[1,128,1024]{2,1,0:T(8,128)(2,1)} copy(bf16[1,128,1024]{2,1,0:T(8,128)(2,1)} %bitcast.12) | data formatting | bytes 524288
  63.9 1.7 %copy.22 = bf16[1,128,1024]{2,1,0:T(8,128)(2,1)} copy(bf16[1,128,1024]{2,1,0:T(8,128)(2,1)} %bitcast.11) | data formatting | bytes 524288
  65.6 0.0 copy-done
  65.6 0.7 %copy.23 = bf16[1,128,1024]{2,1,0:T(8,128)(2,1)} copy(bf16[1,128,1024]{2,1,0:T(8,128)(2,1)S(1)} %bitcast.10) | data formatting | bytes 524288
  66.3 0.0 copy-done.1
  66.3 0.7 copy.24
Async XLA Ops:
  58.9 6.7 %copy-start = (bf16[128,1024]{1,0:T(8,128)(2,1)S(1)}, bf16[128,1024]{1,0:T(8,128)(2,1)}, u32[]{:S(2)}) copy-start(bf16[128,1024]{1,0:T(8,128)(2,1)} %get-tuple-element.16) | copy-start | bytes 786436
  58.9 7.4 %copy-start.1 = (f32[32,1024]{1,0:T(8,128)S(1)}, f32[32,1024]{1,0:T(8,128)}, u32[]{:S(2)}) copy-start(f32[32,1024]{1,0:T(8,128)} %get-tuple-element.29) | copy-start | bytes 393220

commit v4 on v3

--- a/solution.py
+++ b/solution.py
@@ -406,6 +406,19 @@
             level_copy(o, g).wait_send()
     for store in stores:
         store.wait()
+
+
+def hand_over(*refs):
+    count = len(refs) // 2
+    done = refs[-1]
+    copies = [
+        pltpu.make_async_copy(src, dst, done.at[i])
+        for i, (src, dst) in enumerate(zip(refs[:count], refs[count : 2 * count]))
+    ]
+    for copy in copies:
+        copy.start()
+    for copy in copies:
+        copy.wait()
 
 
 def shards(queries, keys, values, gates, cotangent, segment, w_out):
@@ -490,6 +503,15 @@
     )(
         queries[0], keys[0], values[0], gates[0], cotangent[0], w_out, segment,
     )
+    results = pl.pallas_call(
+        hand_over,
+        out_shape=tuple(jax.ShapeDtypeStruct(r.shape, r.dtype) for r in results),
+        in_specs=[anywhere] * 6,
+        out_specs=(anywhere,) * 6,
+        scratch_shapes=[dma((6,))],
+        compiler_params=pltpu.CompilerParams(vmem_limit_bytes=62 * 1024 * 1024),
+        cost_estimate=pl.CostEstimate(flops=0, bytes_accessed=3_000_000, transcendentals=0),
+    )(*results)
     output, dq, dk, dv, dgate, weight_grad = results
     if not fused:
         weight_grad = lax.psum_scatter(weight_grad, ("dp", "seq"), scatter_dimension=0, tiled=True)

time: 67.5 us -> 104 us (1.54)
  Pallas kernels: 58.2 us -> 103 us
  local copies, waits for them, and re-layouts: 8.09 us -> 0 us
    pallas_call x0 -> x1, Pallas kernels: none -> 44.8 us  [shards(): pl.pallas_call(hand_over, out_shape=tuple((jax.ShapeDtypeStruct(r.shape,...]
    unnamed x10 -> x0, local copies, waits for them, and re-layouts: 8.09 us -> none
where the time goes in v4:
time: 104 us
  Pallas kernels  103 us (99%)
    pallas_call x1, Pallas kernels, shards(): pl.pallas_call(functools.partial(kernel, groups, fused), out_shape=(token...  58.2 us
    pallas_call x1, Pallas kernels, shards(): pl.pallas_call(hand_over, out_shape=tuple((jax.ShapeDtypeStruct(r.shape,...  44.8 us

profile of v4, /device:TPU:0, one launch (start us, length us, event | category | flops | bytes accessed | tf_op | source)
XLA Modules:
  0.0 103.7 jit_solution(15031827150343608486)
XLA Ops:
  0.6 58.2 %shard_map.118 = (bf16[128,1024]{1,0:T(8,128)(2,1)}, bf16[128,1024]{1,0:T(8,128)(2,1)}, bf16[128,1024]{1,0:T(8,128)(2,1)}, bf16[128,1024]{1,0:T(8,128)(2,1)}, bf...) custom-call(bf16[128,1024]{1,0:T(8,128)(2,1)} %bitcast.10, bf16[128,1024]{1,0:T(8,128)(2,1)} %bitcast.11, ...), custom_call_target="tpu_custom_call" | custom-call | flops 3000000000 | bytes 12000000 | tf_op jit(solution)/shard_map/pallas_call | solution.py:440
  58.9 44.8 %shard_map.119 = (bf16[128,1024]{1,0:T(8,128)(2,1)}, bf16[128,1024]{1,0:T(8,128)(2,1)}, bf16[128,1024]{1,0:T(8,128)(2,1)}, bf16[128,1024]{1,0:T(8,128)(2,1)}, bf...) custom-call(bf16[128,1024]{1,0:T(8,128)(2,1)} %get-tuple-element.18.refs_0_, bf16[128,1024]{1,0:T(8,128)(2,1)} %get-tuple-element.19.refs_1_, ...), custom_call_target="tpu_custom_call" | custom-call | bytes 3000000 | tf_op jit(solution)/shard_map/pallas_call | solution.py:506
